TPU v7x, 128 devices: a whole 4x4x4 slice. The times are simulated.
128 devices in a mesh: dp: 4 (over z), vocab: 32 (over x, y, core).
Axes of the slice: x: 4, y: 4, z: 4, core: 2. Of those that a mesh axis runs over, the one named last changes fastest.
Arguments:
- hidden: bfloat16 [1152, 16384], P(('dp', 'vocab')), may hold values from -64 to 64
- head: bfloat16 [65536, 16384], P('vocab', 'dp'), may hold values from -1 to 1
- row_scale: float32 [65536], P('vocab'), may hold values from 1 to 8
- live: int32 [4], replicated, may hold values from 1 to 288, 768 in all
- order: int32 [768], replicated, may hold values from 0 to 767, each once
- beam_log_prob: float32 [1152], P('dp'), may hold values from -8 to 8
- token_length: int32 [1152], P('dp'), may hold values from 1 to 63
- div_ids: int32 [768, 16], P('dp'), may hold values from 0 to 65535
Outputs:
- scored: float32 [768, 65536], P('dp', 'vocab')
- slot_log_normalizer: float32 [1152], P('dp')
Inputs may be any that keep to these rules, and one draw needn't show every extreme that they name: order is a permutation; entry k numbers a live beam, counting replica by replica; live beam w of a replica sits in its slot (w mod 32) * 9 + floor(w / 32).
All inputs are finite; a program needn't handle non-finite values.
Results may differ from a plain program's by a relative error of at most 0.0003.
Values may be sent and summed in bfloat16 or wider, within the bound.
A program may use at most 128 MiB of HBM per device.

v0:
```python
import jax
import jax.numpy as jnp
from jax import lax
from jax.sharding import PartitionSpec as P


def project_rows(rows, head):
    return lax.dot_general(rows, head, (((1,), (1,)), ((), ())), preferred_element_type=jnp.float32)


def per_device(hidden, head, row_scale, live, order, beam_log_prob, token_length, div_ids):
    groups = lax.axis_size("dp")
    shards = lax.axis_size("vocab")
    group = lax.axis_index("dp")
    shard_id = lax.axis_index("vocab")
    local_rows = hidden.shape[0]
    slots = beam_log_prob.shape[0]
    group_rows = div_ids.shape[0]
    voc_local = head.shape[0]
    ends = jnp.cumsum(live)
    starts = ends - live
    replica = jnp.sum((order[:, None] >= ends[None, :]).astype(jnp.int32), axis=1)
    within = order - jnp.take(starts, replica)
    lane_of = within % shards
    depth = within // shards
    slot_position = replica * slots + lane_of * local_rows + depth
    place = lane_of * (groups * local_rows) + replica * local_rows + depth
    quarter = lax.all_to_all(hidden, "dp", split_axis=1, concat_axis=0, tiled=True)
    length_factor = ((5.0 + token_length.astype(jnp.float32)) / 6.0) ** 0.8
    state = lax.all_gather(jnp.stack([beam_log_prob, length_factor]), "dp", axis=1, tiled=True)
    every_row = lax.all_gather(quarter, "vocab", axis=0, tiled=True)
    picked = jnp.take(every_row, place, axis=0)
    mine = lax.psum_scatter(project_rows(picked, head), "dp", scatter_dimension=0, tiled=True)
    logits = mine * row_scale[None, :]
    local_top = jnp.max(logits, axis=1)
    top = lax.pmax(local_top, "vocab")
    total = lax.psum(jnp.sum(jnp.exp(logits - top[:, None]), axis=1), "vocab")
    log_sum_exponent = top + jnp.log(total)
    my_slots = lax.dynamic_slice_in_dim(slot_position, group * group_rows, group_rows, 0)
    my_score = jnp.take(state[0], my_slots)
    my_factor = jnp.take(state[1], my_slots)
    columns = shard_id * voc_local + jnp.arange(voc_local, dtype=jnp.int32)
    count = jnp.sum((div_ids[:, :, None] == columns[None, None, :]).astype(jnp.float32), axis=1)
    scored = (my_score[:, None] + logits - log_sum_exponent[:, None] - 0.5 * count) / my_factor[
        :, None
    ]
    every_lse = lax.all_gather(log_sum_exponent, "dp", axis=0, tiled=True)
    home = jnp.zeros((slots * groups,), jnp.float32).at[slot_position].set(every_lse)
    slot_log_normalizer = lax.dynamic_slice_in_dim(home, group * slots, slots, 0)
    return (scored, slot_log_normalizer)


def solution(mesh):
    return jax.shard_map(
        per_device,
        mesh=mesh,
        in_specs=(
            P(("dp", "vocab"), None),
            P("vocab", "dp"),
            P("vocab"),
            P(),
            P(),
            P("dp"),
            P("dp"),
            P("dp", None),
        ),
        out_specs=(P("dp", "vocab"), P("dp")),
        check_vma=False,
    )
```

profile of v0, /device:TPU:0, one launch (start us, length us, event | category | flops | bytes accessed | tf_op | source)
XLA Modules:
  0.0 348.8 jit_solution(2612938191109524193)
XLA Ops:
  7.2 1.2 all_to_all.14
  8.5 0.2 copy.18
  8.6 14.7 %all_to_all.19 = bf16[9,4,4096]{2,0,1:T(8,128)(2,1)S(1)} all-to-all(bf16[9,4,4096]{2,0,1:T(8,128)(2,1)S(1)} %copy.18), channel_id=1, replica_groups=mesh['dp'=4,'vocab'=32] {'dp'}, dimensions={1} | all-to-all | bytes 589824 | tf_op jit(solution)/shard_map/all_to_all | solution.py:28
  23.3 0.8 reshape.136
  24.2 0.2 reduce-window.8
  24.4 0.7 fusion.11
  25.1 0.1 convert_reduce_fusion.1
  25.2 2.6 fusion.7
  27.8 53.8 %all-gather.4.cloned.1.call-done = bf16[32,36,4096]{2,1,0:T(8,128)(2,1)} async-done(((bf16[1,36,4096]{2,1,0:T(8,128)(2,1)}), bf16[32,36,4096]{2,1,0:T(8,128)(2,1)}) %all-gather.4.cloned.1.call-update) | async-done | bytes 9437200 | tf_op jit(solution)/shard_map/all_gather | solution.py:31
  81.6 13.2 %reshape.137 = bf16[1152,4096]{1,0:T(8,128)(2,1)} reshape(bf16[32,36,4096]{2,1,0:T(8,128)(2,1)} %all-gather.4.cloned.1.call-done) | data formatting | bytes 18874368
  94.8 16.9 %gather_fusion = bf16[768,4096]{1,0:T(8,128)(2,1)} fusion(bf16[1152,4096]{1,0:T(8,128)(2,1)} %reshape.137, s32[1024]{0:T(1024)S(1)} %pad_clamp_fusion), kind=kCustom, calls=%fused_computation.2 | custom fusion | bytes 12585984 | tf_op jit(solution)/shard_map/jit(_take)/gather | solution.py:32
  111.6 20.4 %fusion = f32[768,2048]{1,0:T(8,128)} fusion(bf16[2048,4096]{1,0:T(8,128)(2,1)} %param.11, bf16[768,4096]{1,0:T(8,128)(2,1)} %gather_fusion, pred[768]{0:T(1024)(128)(4,1)S(1)} %get-tuple-element.9), kind=kOutput, calls=%fused_computation.5 | convolution fusion | flops 12888047616 | bytes 29360896 | tf_op jit(solution)/shard_map/dot_general | solution.py:8
  132.0 0.6 copy-done.5
  132.7 12.5 %all-gather = f32[4,288,2]{1,2,0:T(2,128)S(1)} all-gather(f32[1,288,2]{1,2,0:T(2,128)S(1)} %maximum_bitcast_fusion), channel_id=1, replica_groups=mesh['dp'=4,'vocab'=32] {'dp'}, dimensions={0}, use_global_device_ids=true | all-gather | bytes 11520 | tf_op jit(solution)/shard_map/all_gather | solution.py:30
  145.2 0.1 reshape.135
  145.3 0.1 compare_select_fusion.7
  145.5 1.4 gather_fusion.1
  146.9 1.4 gather_fusion.2
  148.4 0.1 copy.19
  148.5 0.6 dynamic-slice
  149.8 0.1 broadcast_select_fusion.1
  149.8 5.1 %convert_reduce_fusion = f32[192,2048]{1,0:T(8,128)S(1)} fusion(s32[2048]{0:T(1024)S(1)} %iota_add_fusion, s32[192,16]{1,0:T(8,128)S(1)} %copy.19), kind=kLoop, calls=%fused_computation.4 | loop fusion | flops 18481152 | bytes 1593344 | tf_op jit(solution)/shard_map/reduce_sum | solution.py:43
  155.0 41.0 %reduce-scatter.2.cloned.1.call-done = f32[192,2048]{1,0:T(8,128)} async-done(((f32[768,2048]{1,0:T(8,128)}), f32[192,2048]{1,0:T(8,128)}) %reduce-scatter.2.cloned.1.call-update) | async-done | bytes 1572880 | tf_op jit(solution)/shard_map/reduce_scatter | solution.py:33
  196.0 1.7 multiply_reduce_fusion
  197.7 67.0 %pmax.7 = f32[192]{0:T(256)S(1)} all-reduce(f32[192]{0:T(256)S(1)} %multiply_reduce_fusion), channel_id=1, replica_groups=mesh['dp'=4,'vocab'=32] {'vocab'}, use_global_device_ids=true, to_apply=%region_4.6 | all-reduce | flops 192 | bytes 1536 | tf_op jit(solution)/shard_map/pmax | solution.py:36
  264.7 0.4 exponential_reduce_fusion
  265.1 62.7 %psum.7 = f32[192]{0:T(256)S(1)} all-reduce(f32[192]{0:T(256)S(1)} %exponential_reduce_fusion), channel_id=1, replica_groups=mesh['dp'=4,'vocab'=32] {'vocab'}, use_global_device_ids=true, to_apply=%region_6.8 | all-reduce | flops 192 | bytes 1536 | tf_op jit(solution)/shard_map/psum | solution.py:37
  327.7 0.1 fusion.10
  327.8 8.5 %all-reduce = f32[768]{0:T(1024)S(1)} all-reduce(f32[768]{0:T(1024)S(1)} %get-tuple-element.5), channel_id=1, replica_groups=mesh['dp'=4,'vocab'=32] {'dp'}, use_global_device_ids=true, to_apply=%add | all-reduce | flops 768 | bytes 6144
  336.4 3.4 scatter_custom_fusion
  339.7 0.7 dynamic_slice.7
  340.4 1.6 subtract_divide_fusion
  (32 shorter events, 0.3 us)
Async XLA Ops:
  7.2 74.4 %all-gather.4.cloned.1.call-start = ((), (), s32[]{:S(2)}) async-start(), calls=%async_computation.3 | async-start | bytes 10813440 | tf_op jit(solution)/shard_map/all_gather | solution.py:31
  8.4 15.8 %copy-start.6 = (s32[4]{0:T(128)S(1)}, s32[4]{0:T(128)}, u32[]{:S(2)}) copy-start(s32[4]{0:T(128)} %param.13) | copy-start | bytes 52
  8.4 16.6 %copy-start.2 = (s32[768]{0:T(1024)S(1)}, s32[768]{0:T(1024)}, u32[]{:S(2)}) copy-start(s32[768]{0:T(1024)} %param.14) | copy-start | bytes 9220
  24.2 171.8 %reduce-scatter.2.cloned.1.call-start = ((), (), s32[]{:S(2)}) async-start(), calls=%async_computation.2 | async-start | bytes 7864320 | tf_op jit(solution)/shard_map/reduce_scatter | solution.py:33
  132.0 0.7 copy-start.5
  132.0 0.7 copy-start.4
  132.0 16.4 %copy-start.3 = (s32[192,16]{0,1:T(8,128)S(1)}, s32[192,16]{0,1:T(8,128)}, u32[]{:S(2)}) copy-start(s32[192,16]{0,1:T(8,128)} %param.17) | copy-start | bytes 36868
  132.0 16.5 %copy-start.7 = (u32[128]{0:T(128)S(1)}, u32[128]{0:T(128)}, u32[]{:S(2)}) copy-start(u32[128]{0:T(128)} %constant.118) | copy-start | bytes 1540
  146.9 49.0 %copy-start.1 = (f32[2048]{0:T(1024)S(1)}, f32[2048]{0:T(1024)}, u32[]{:S(2)}) copy-start(f32[2048]{0:T(1024)} %param.12) | copy-start | bytes 24580
  196.0 68.7 %copy-start = (f32[192,2048]{1,0:T(8,128)S(1)}, f32[192,2048]{1,0:T(8,128)}, u32[]{:S(2)}) copy-start(f32[192,2048]{1,0:T(8,128)} %reduce-scatter.2.cloned.1.call-done) | copy-start | bytes 4718596
Sparse Core Ops, SparseCore 0:
  24.3 57.2 all-gather.3
  132.1 63.7 reduce-scatter.1
where the time goes:
time: 350 us; the launch traced here: 349 us
  blocking collectives  165 us (47%)
  waiting for transfers between devices  94.8 us (27%)
  local copies, waits for them, and re-layouts  41.4 us (12%)
  matrix products  20.4 us (6%)
  between operations  14.9 us (4%)
  other arithmetic  12 us (3%)
    pmax x1, blocking collectives, per_device(): top = lax.pmax(local_top, 'vocab')  67 us
    psum x1, blocking collectives, per_device(): total = lax.psum(jnp.sum(jnp.exp(logits - top[:, None]), axis=1), 'vocab')  62.7 us
    all_gather x1, waiting for transfers between devices, per_device(): every_row = lax.all_gather(quarter, 'vocab', axis=0, tiled=True)  53.8 us
    reduce_scatter x1, waiting for transfers between devices, per_device(): lax.psum_scatter(project_rows(picked, head), 'dp', scatter_dimension=0, t...  41 us
    dot_general x1, matrix products, project_rows(): lax.dot_general(rows, head, (((1,), (1,)), ((), ())), preferred_element_t...  20.4 us
    gather x1, local copies, waits for them, and re-layouts, per_device(): picked = jnp.take(every_row, place, axis=0)  16.9 us
    unnamed x22, local copies, waits for them, and re-layouts  15.5 us
    all_to_all x1, blocking collectives, per_device(): lax.all_to_all(hidden, 'dp', split_axis=1, concat_axis=0, tiled=True)  14.7 us
  transfers between devices with their start and end apart: 2, of which 2 were waited for; matrix products, arithmetic and copies ran while one was open for 4% of the time, Pallas kernels for 0%

commit v1 on v0

v1 whole, which is shorter than its diff:
```python
import functools

import jax
import jax.numpy as jnp
from jax import lax
from jax.experimental import pallas as pl
from jax.experimental.pallas import tpu as pltpu
from jax.sharding import PartitionSpec as P

F32, BF16, I32, I16 = jnp.float32, jnp.bfloat16, jnp.int32, jnp.int16
MESH = pl.DeviceIdType.MESH

STEPS_ANY = ((4, 0, 48), (4, 48, 96), (4, 96, 144), (4, 144, 192))
CAP = 32
RB = 16


def iota(shape, axis):
    return lax.broadcasted_iota(I32, shape, axis)


def to_col(row, n, shift=0):
    width = row.shape[1]
    hit = iota((n, width), 0) + shift == iota((n, width), 1)
    return jnp.sum(jnp.where(hit, row, jnp.zeros_like(row)), axis=1, keepdims=True)


def to_row(col, width, shift=0):
    n = col.shape[0]
    hit = iota((n, width), 0) + shift == iota((n, width), 1)
    return jnp.sum(jnp.where(hit, col, jnp.zeros_like(col)), axis=0, keepdims=True)


def live_of_lane(count, lane):
    return (count - lane + 31) >> 5


def row_info(order, live):
    e0 = live[0]
    e1 = e0 + live[1]
    e2 = e1 + live[2]
    past = [(order >= e).astype(I32) for e in (e0, e1, e2)]
    replica = past[0] + past[1] + past[2]
    within = order - (past[0] * live[0] + past[1] * live[1] + past[2] * live[2])
    lane, depth = within & 31, within >> 5
    row = depth
    for i in range(3):
        row = row + past[i] * live_of_lane(live[i], lane)
    return replica, lane, depth, row


def place(lane, x, y):
    lx, ly, lc = lane >> 3, (lane >> 1) & 3, lane & 1
    dx, dy = (lx - x) & 3, (ly - y) & 3
    r1 = dx + lc * (dy - dx)
    r2 = dy + lc * (dx - dy)
    g1, g2 = r1 ^ (r1 >> 1), r2 ^ (r2 >> 1)
    near = (g2 == 1) | (g2 == 2)
    chunk = jnp.where(g2 == 0, 0, jnp.where(g2 == 3, 3, 1 + (g1 >> 1)))
    minor = jnp.where(near, (g2 - 1) * 2 + (g1 & 1), g1)
    return chunk, chunk * 8 + lc * 4 + minor


def quantize(val):
    top = jnp.maximum(jnp.max(jnp.abs(val), axis=1, keepdims=True), 1e-30)
    coded = jnp.round(val * (32767.0 / top)).astype(I32).astype(I16)
    return coded, top * (1.0 / 32767.0)


def widen(coded):
    return coded.astype(I32).astype(F32)


def kernel(steps, by_arrival,
           hidden, head, row_scale, live, order, blp, tlen, div,
           scored, slotn,
           hrecv, pool, headv, st, pos, sel, xsel, S,
           SP, SM, RM, RP, SP2, SM2, RM2, RP2,
           CP, CM, KM, KP, CP2, CM2, KM2, KP2,
           TA, TB, LS,
           head_sem, own_sem, z_s, z_r, t_s, t_r,
           r1_s, r1_r, r2_s, r2_r, sib_s, sib_r,
           rs_s, rs_r, ta_s, ta_r, tb_s, tb_r, ls_s, ls_r):
    q = lax.axis_index("dp")
    v = lax.axis_index("vocab")
    x, y, c = v // 8, (v // 2) % 4, v % 2
    width = hidden.shape[1] // 4
    half_v = head.shape[0] // 2
    voc = head.shape[0]
    rows_g = order.shape[1]
    slots = blp.shape[1]
    n_steps = len(steps)

    def dev(zz, xx, yy, cc):
        return (zz % 4, (xx % 4) * 8 + (yy % 4) * 2 + (cc % 2))

    zdev = [dev(q + d, x, y, c) for d in range(4)]
    fan = [(dy, dc) for dy in range(4) for dc in range(2)]
    adev = [dev(q, x, y + dy, c + dc) for dy, dc in fan]
    bdev = [dev(q, x + d, y, c) for d in range(4)]
    sibling = adev[1]
    r1p = dev(q, x + (1 - c), y + c, c)
    r1m = dev(q, x + 3 * (1 - c), y + 3 * c, c)
    r2p = dev(q, x + c, y + (1 - c), c)
    r2m = dev(q, x + 3 * c, y + 3 * (1 - c), c)
    sends = []

    def rc(src, dst, ss, rs, device):
        return pltpu.make_async_remote_copy(
            src_ref=src, dst_ref=dst, send_sem=ss, recv_sem=rs, device_id=device, device_id_type=MESH)

    def push(src, dst, ss, rs, device):
        copy = rc(src, dst, ss, rs, device)
        copy.start()
        sends.append(copy)

    def got(dst, rs):
        rc(dst, dst, z_s.at[0], rs, zdev[1]).wait_recv()

    head_copy = pltpu.make_async_copy(head, headv, head_sem)
    head_copy.start()
    own_copy = pltpu.make_async_copy(
        hidden.at[:, pl.ds(pl.multiple_of(q * width, width), width)], hrecv.at[q], own_sem)
    own_copy.start()
    st[q] = jnp.zeros(st.shape[1:], F32)
    st[q, 0:1, 0:slots] = blp[...]
    st[q, 1:2, 0:slots] = jnp.exp(0.8 * jnp.log((5.0 + tlen[...].astype(F32)) / 6.0))
    for ref in (CP, CM, CP2, CM2):
        ref[...] = jnp.zeros(ref.shape, F32)
    TA[0] = jnp.zeros(TA.shape[1:], F32)
    TB[0] = jnp.zeros(TB.shape[1:], F32)
    LS[q] = jnp.zeros(LS.shape[1:], F32)

    barrier = pltpu.get_barrier_semaphore()
    peers = zdev[1:] + adev[1:] + bdev[1:]
    for device in peers:
        pl.semaphore_signal(barrier, inc=1, device_id=device, device_id_type=MESH)
    pl.semaphore_wait(barrier, len(peers))

    for d in (2, 1, 3):
        to = (q + d) % 4
        push(hidden.at[:, pl.ds(pl.multiple_of(to * width, width), width)], hrecv.at[q],
             z_s.at[d - 1], z_r.at[d - 1], zdev[d])
    for d in (1, 2, 3):
        push(st.at[q], st.at[q], t_s.at[d - 1], t_r.at[d - 1], zdev[d])

    groups = [(q + 2) % 4, (q + 1) % 4, (q + 3) % 4, q]
    own_rank = None
    for gi in range(4):
        o = order[pl.ds(groups[gi], 1), :]
        replica, lane, depth, row = row_info(o, live)
        chunk, block = place(lane, x, y)
        where_row = block * CAP + row
        if by_arrival:
            key = chunk * 256 + iota((1, rows_g), 1)
            rank = jnp.sum((to_col(key, rows_g) < key).astype(I32), axis=0, keepdims=True)
        else:
            rank = iota((1, rows_g), 1)
        hit = iota((rows_g, rows_g), 0) == rank
        col = jnp.sum(jnp.where(hit, where_row, 0), axis=1, keepdims=True)
        pos[gi * rows_g:(gi + 1) * rows_g, :] = jnp.broadcast_to(col, (rows_g, 128))
        own_rank = rank

    own_copy.wait()
    for d in (1, 3, 2):
        got(hrecv.at[(q + 4 - d) % 4], z_r.at[d - 1])
    counts = [live_of_lane(live[r], v) for r in range(4)]
    picks = []
    first = 0
    for r in range(4):
        i, j = iota((CAP, 9), 0), iota((CAP, 9), 1)
        picks.append(jnp.where((i == first + j) & (j < counts[r]), 1.0, 0.0).astype(BF16))
        first = first + counts[r]

    def blk(idx):
        return pool.at[pl.ds(pl.multiple_of(idx * CAP, CAP), CAP), :]

    def half(idx, h):
        return pool.at[pl.ds(pl.multiple_of(idx * CAP + h * (CAP // 2), CAP // 2), CAP // 2), :]

    t4 = 4 * c
    u4 = 4 - t4
    span = 1024
    for k in range(width // span):
        cols = slice(k * span, (k + 1) * span)
        acc = jnp.zeros((CAP, span), F32)
        for r in range(4):
            acc += jnp.dot(picks[r], hrecv[r, :, cols], preferred_element_type=F32)
        pool[pl.ds(pl.multiple_of(t4 * CAP, CAP), CAP), cols] = acc.astype(BF16)

    def to_sibling(ch, m):
        push(blk(ch * 8 + t4 + m), blk(ch * 8 + t4 + m), sib_s.at[ch * 4 + m], sib_r.at[ch * 4 + m], sibling)

    def from_sibling(ch):
        for m in range(4):
            got(blk(ch * 8 + u4 + m), sib_r.at[ch * 4 + m])

    def spread(m):
        ch, mm = 1 + (m >> 1), m & 1
        push(blk(t4 + m), blk(ch * 8 + t4 + 2 + mm), r2_s.at[2 * m + 1], r2_r.at[2 * m + 1], r2p)
        push(blk(t4 + m), blk(ch * 8 + t4 + mm), r2_s.at[2 * m], r2_r.at[2 * m], r2m)

    def gather_chunk(ch):
        if ch == 0:
            push(blk(t4), blk(t4 + 2), r1_s.at[1], r1_r.at[1], r1p)
            push(blk(t4), blk(t4 + 1), r1_s.at[0], r1_r.at[0], r1m)
            to_sibling(0, 0)
            spread(0)
            got(blk(t4 + 1), r1_r.at[0])
            push(half(t4 + 1, 0), half(t4 + 3, 0), r1_s.at[2], r1_r.at[2], r1m)
            got(blk(t4 + 2), r1_r.at[1])
            push(half(t4 + 2, 1), half(t4 + 3, 1), r1_s.at[3], r1_r.at[3], r1p)
            to_sibling(0, 1)
            to_sibling(0, 2)
            spread(1)
            spread(2)
            got(half(t4 + 3, 0), r1_r.at[2])
            got(half(t4 + 3, 1), r1_r.at[3])
            to_sibling(0, 3)
            spread(3)
        elif ch < 3:
            for mm in range(2):
                m = 2 * (ch - 1) + mm
                got(blk(ch * 8 + t4 + mm), r2_r.at[2 * m])
                push(half(ch * 8 + t4 + mm, 0), half(24 + t4 + m, 0), r2_s.at[8 + 2 * m], r2_r.at[8 + 2 * m], r2m)
                to_sibling(ch, mm)
                got(blk(ch * 8 + t4 + 2 + mm), r2_r.at[2 * m + 1])
                push(half(ch * 8 + t4 + 2 + mm, 1), half(24 + t4 + m, 1),
                     r2_s.at[9 + 2 * m], r2_r.at[9 + 2 * m], r2p)
                to_sibling(ch, 2 + mm)
        else:
            for m in range(4):
                got(half(24 + t4 + m, 0), r2_r.at[8 + 2 * m])
                got(half(24 + t4 + m, 1), r2_r.at[9 + 2 * m])
                to_sibling(3, m)
        from_sibling(ch)

    def multiply(s):
        n_ch, lo, hi = steps[s]
        m = hi - lo
        wide = n_ch * 8 * CAP
        for gi in range(4):
            at = pos[gi * rows_g + lo:gi * rows_g + hi, :]
            for b in range(wide // 128):
                hit = at == iota((m, 128), 1) + 128 * b
                sel[gi * m:(gi + 1) * m, b * 128:(b + 1) * 128] = jnp.where(hit, 1.0, 0.0).astype(BF16)

        @pl.loop(0, width // 512)
        def _(n):
            cols = pl.ds(pl.multiple_of(n * 512, 512), 512)
            xsel[0:4 * m, cols] = jnp.dot(
                sel[0:4 * m, 0:wide], pool[0:wide, cols], preferred_element_type=F32).astype(BF16)

        if s == 0:
            head_copy.wait()

        @pl.loop(0, voc // 256)
        def _(n):
            cols = pl.ds(pl.multiple_of(n * 256, 256), 256)
            out = lax.dot_general(xsel[0:4 * m, :], headv[cols, :], (((1,), (1,)), ((), ())),
                                  preferred_element_type=F32)
            for gi in range(4):
                S[gi * rows_g + lo:gi * rows_g + hi, cols] = out[gi * m:(gi + 1) * m, :]

    def blocks(s, body):
        _, lo, hi = steps[s]

        @pl.loop(0, (hi - lo) // RB)
        def _(b):
            shift = pl.multiple_of(b * RB, RB)
            body(shift, pl.multiple_of(lo + shift, RB))

    H0, H1 = slice(0, half_v), slice(half_v, 2 * half_v)

    def rows_of(gi, rows):
        return pl.ds(pl.multiple_of(gi * rows_g + rows, RB), RB)

    def send_first(s):
        _, lo, hi = steps[s]

        def body(shift, rows):
            r = pl.ds(rows, RB)
            for buf, scales, line, gi, src, dst in (
                    (SP, CP, 0, 0, H0, H0), (SM, CM, 1, 0, H1, H1),
                    (SP, CP, 1, 1, H1, H1), (SM, CM, 0, 2, H0, H0)):
                coded, scale = quantize(S[rows_of(gi, rows), src])
                buf[r, dst] = coded
                scales[s, line:line + 1, :] += to_row(scale, 128, shift)

        blocks(s, body)
        push(SP.at[lo:hi, :], RM.at[lo:hi, :], rs_s.at[s, 0], rs_r.at[s, 0], zdev[1])
        push(SM.at[lo:hi, :], RP.at[lo:hi, :], rs_s.at[s, 1], rs_r.at[s, 1], zdev[3])
        push(CP.at[s], KM.at[s], rs_s.at[s, 2], rs_r.at[s, 2], zdev[1])
        push(CM.at[s], KP.at[s], rs_s.at[s, 3], rs_r.at[s, 3], zdev[3])

    def send_second(s):
        _, lo, hi = steps[s]
        got(RM.at[lo:hi, :], rs_r.at[s, 0])
        got(RP.at[lo:hi, :], rs_r.at[s, 1])
        got(KM.at[s], rs_r.at[s, 2])
        got(KP.at[s], rs_r.at[s, 3])

        def body(shift, rows):
            r = pl.ds(rows, RB)
            for buf, scales, recv, rscale, line, gi, cols in (
                    (SP2, CP2, RM, KM, 0, 1, H0), (SM2, CM2, RP, KP, 1, 2, H1)):
                old = widen(recv[r, cols]) * to_col(rscale[s, line:line + 1, :], RB, shift)
                coded, scale = quantize(S[rows_of(gi, rows), cols] + old)
                buf[r, :] = coded
                scales[s, 0:1, :] += to_row(scale, 128, shift)

        blocks(s, body)
        push(SP2.at[lo:hi, :], RM2.at[lo:hi, :], rs_s.at[s, 4], rs_r.at[s, 4], zdev[1])
        push(SM2.at[lo:hi, :], RP2.at[lo:hi, :], rs_s.at[s, 5], rs_r.at[s, 5], zdev[3])
        push(CP2.at[s], KM2.at[s], rs_s.at[s, 6], rs_r.at[s, 6], zdev[1])
        push(CM2.at[s], KP2.at[s], rs_s.at[s, 7], rs_r.at[s, 7], zdev[3])

    def finish(s):
        _, lo, hi = steps[s]
        got(RM2.at[lo:hi, :], rs_r.at[s, 4])
        got(RP2.at[lo:hi, :], rs_r.at[s, 5])
        got(KM2.at[s], rs_r.at[s, 6])
        got(KP2.at[s], rs_r.at[s, 7])

        def body(shift, rows):
            r = pl.ds(rows, RB)
            mine = rows_of(3, rows)

            def col(ref, line):
                return to_col(ref[s, line:line + 1, :], RB, shift)

            l0 = (S[mine, H0] + widen(RM2[r, :]) * col(KM2, 0) + widen(RP[r, H0]) * col(KP, 0)) * row_scale[:, H0]
            l1 = (S[mine, H1] + widen(RP2[r, :]) * col(KP2, 0) + widen(RM[r, H1]) * col(KM, 1)) * row_scale[:, H1]
            S[mine, H0] = l0
            S[mine, H1] = l1
            top = jnp.maximum(jnp.max(l0, axis=1, keepdims=True), jnp.max(l1, axis=1, keepdims=True))
            total = jnp.sum(jnp.exp(l0 - top), axis=1, keepdims=True) + jnp.sum(jnp.exp(l1 - top), axis=1, keepdims=True)
            TA[0, 0:1, :] += to_row(top, 256, rows)
            TA[0, 1:2, :] += to_row(total, 256, rows)

        blocks(s, body)

    done_ch = 0
    for s in range(n_steps):
        while done_ch < steps[s][0]:
            gather_chunk(done_ch)
            done_ch += 1
        multiply(s)
        send_first(s)
        if s >= 1:
            send_second(s - 1)
        if s >= 2:
            finish(s - 2)

    base = v * voc

    @pl.loop(0, rows_g // RB)
    def _(b):
        r = pl.ds(pl.multiple_of(b * RB, RB), RB)
        ids = div[r, :] - base
        for k in range(voc // 512):
            token = iota((RB, 512), 1) + k * 512
            acc = jnp.zeros((RB, 512), F32)
            for j in range(16):
                acc = acc - jnp.where(ids[:, j:j + 1] == token, 0.5, 0.0)
            scored[r, k * 512:(k + 1) * 512] = acc

    send_second(n_steps - 1)

    for d in (1, 2, 3):
        got(st.at[(q + 4 - d) % 4], t_r.at[d - 1])
    replica, lane, depth, _ = row_info(order[pl.ds(q, 1), :], live)
    slot_col = to_col(replica * slots + lane * 9 + depth, rows_g)
    rank_col = to_col(own_rank, rows_g)
    score = jnp.zeros((rows_g, 1), F32)
    factor = jnp.zeros((rows_g, 1), F32)
    for r in range(4):
        hit = slot_col - r * slots == iota((rows_g, st.shape[2]), 1)
        score += jnp.sum(jnp.where(hit, st[r, 0:1, :], 0.0), axis=1, keepdims=True)
        factor += jnp.sum(jnp.where(hit, st[r, 1:2, :], 0.0), axis=1, keepdims=True)
    inverse = 1.0 / factor
    perm = rank_col == iota((rows_g, 256), 1)
    permute = jnp.where(rank_col == iota((rows_g, rows_g), 1), 1.0, 0.0)

    if n_steps >= 2:
        finish(n_steps - 2)
    finish(n_steps - 1)

    for i in range(1, 8):
        push(TA.at[0], TA.at[i], ta_s.at[i], ta_r.at[i], adev[i])

    @pl.loop(0, voc // 256)
    def _(n):
        cols = pl.ds(pl.multiple_of(n * 256, 256), 256)
        scored[:, cols] += jnp.dot(permute, S[3 * rows_g:4 * rows_g, cols], precision=lax.Precision.HIGHEST,
                                   preferred_element_type=F32)

    def combine(ref, n):
        tops = [ref[i, 0:1, :] for i in range(n)]
        top = functools.reduce(jnp.maximum, tops)
        total = sum(ref[i, 1:2, :] * jnp.exp(tops[i] - top) for i in range(n))
        return top, total

    for i in range(1, 8):
        got(TA.at[i], ta_r.at[i])
    top, total = combine(TA, 8)
    TB[0, 0:1, :] = top
    TB[0, 1:2, :] = total
    for i in range(1, 4):
        push(TB.at[0], TB.at[i], tb_s.at[i], tb_r.at[i], bdev[i])
    for i in range(1, 4):
        got(TB.at[i], tb_r.at[i])
    top, total = combine(TB, 4)
    lse_rank = top + jnp.log(total)
    lse = jnp.sum(jnp.where(perm, lse_rank, 0.0), axis=1, keepdims=True)
    LS[q, 0:1, :] = to_row(lse, 256)
    for d in (1, 2, 3):
        push(LS.at[q], LS.at[q], ls_s.at[d - 1], ls_r.at[d - 1], zdev[d])
    shift_col = score - lse
    for k in range(voc // 256):
        cols = slice(k * 256, (k + 1) * 256)
        scored[:, cols] = (scored[:, cols] + shift_col) * inverse

    for d in (1, 2, 3):
        got(LS.at[(q + 4 - d) % 4], ls_r.at[d - 1])
    acc = jnp.zeros((1, st.shape[2]), F32)
    for g in range(4):
        replica, lane, depth, _ = row_info(order[g:g + 1, :], live)
        slot_col = to_col(replica * slots + lane * 9 + depth, rows_g)
        lse_col = to_col(LS[g, 0:1, :], rows_g)
        hit = slot_col - q * slots == iota((rows_g, st.shape[2]), 1)
        acc += jnp.sum(jnp.where(hit, lse_col, 0.0), axis=0, keepdims=True)
    slotn[...] = acc[:, 0:slots]

    for copy in sends:
        copy.wait_send()


def call(steps, by_arrival, ident, hidden, head, row_scale, live, order, blp, tlen, div):
    rows_g, voc, width, slots = order.shape[1], head.shape[0], head.shape[1], blp.shape[1]
    half_v = voc // 2
    n = len(steps)
    tall = 4 * max(hi - lo for _, lo, hi in steps)
    dma = pltpu.SemaphoreType.DMA
    vmem = pl.BlockSpec(memory_space=pltpu.VMEM)
    anyspace = pl.BlockSpec(memory_space=pl.ANY)
    smem = pl.BlockSpec(memory_space=pltpu.SMEM)
    return pl.pallas_call(
        functools.partial(kernel, steps, by_arrival),
        out_shape=(jax.ShapeDtypeStruct((rows_g, voc), F32), jax.ShapeDtypeStruct((1, slots), F32)),
        in_specs=[anyspace, anyspace, vmem, smem, vmem, vmem, vmem, vmem],
        out_specs=(vmem, vmem),
        scratch_shapes=[
            pltpu.VMEM((4, hidden.shape[0], width), BF16),
            pltpu.VMEM((32 * CAP, width), BF16),
            pltpu.VMEM((voc, width), BF16),
            pltpu.VMEM((4, 8, 384), F32),
            pltpu.VMEM((4 * rows_g, 128), I32),
            pltpu.VMEM((tall, 32 * CAP), BF16),
            pltpu.VMEM((tall, width), BF16),
            pltpu.VMEM((4 * rows_g, voc), F32),
            *[pltpu.VMEM((rows_g, voc), I16)] * 4,
            *[pltpu.VMEM((rows_g, half_v), I16)] * 4,
            *[pltpu.VMEM((n, 8, 128), F32)] * 8,
            pltpu.VMEM((8, 8, 256), F32),
            pltpu.VMEM((4, 8, 256), F32),
            pltpu.VMEM((4, 8, 256), F32),
            dma, dma,
            dma((3,)), dma((3,)), dma((3,)), dma((3,)),
            dma((4,)), dma((4,)), dma((16,)), dma((16,)), dma((16,)), dma((16,)),
            dma((n, 8)), dma((n, 8)), dma((8,)), dma((8,)), dma((4,)), dma((4,)), dma((3,)), dma((3,)),
        ],
        compiler_params=pltpu.CompilerParams(
            collective_id=ident, has_side_effects=True, vmem_limit_bytes=60 * 1024 * 1024),
    )(hidden, head, row_scale, live, order, blp, tlen, div)


def per_device(hidden, head, row_scale, live, order, beam_log_prob, token_length, div_ids):
    groups = lax.axis_size("dp")
    scored, slot = call(
        STEPS_ANY, False, 0, hidden, head, row_scale[None, :], live, order.reshape(groups, -1),
        beam_log_prob[None, :], token_length[None, :], div_ids)
    return scored, slot[0]


def solution(mesh):
    return jax.shard_map(
        per_device,
        mesh=mesh,
        in_specs=(
            P(("dp", "vocab"), None),
            P("vocab", "dp"),
            P("vocab"),
            P(),
            P(),
            P("dp"),
            P("dp"),
            P("dp", None),
        ),
        out_specs=(P("dp", "vocab"), P("dp")),
        check_vma=False,
    )
```

time: 350 us -> 123 us (0.35)
  blocking collectives: 165 us -> 0 us
  Pallas kernels: 0 us -> 113 us
  waiting for transfers between devices: 94.8 us -> 0 us
  local copies, waits for them, and re-layouts: 41.4 us -> 8.02 us
  matrix products: 20.4 us -> 0 us
  between operations: 14.9 us -> 0.64 us
  other arithmetic: 12 us -> 1.25 us
    pallas_call x0 -> x1, Pallas kernels: none -> 113 us  [call(): pl.pallas_call(functools.partial(kernel, steps, by_arrival), out_shape=(j...]
    pmax x1 -> x0, blocking collectives: 67 us -> none  [per_device(): top = lax.pmax(local_top, 'vocab')]
    psum x1 -> x0, blocking collectives: 62.7 us -> none  [per_device(): total = lax.psum(jnp.sum(jnp.exp(logits - top[:, None]), axis=1), 'vocab')]
    all_gather x1 -> x0, waiting for transfers between devices: 53.8 us -> none  [per_device(): every_row = lax.all_gather(quarter, 'vocab', axis=0, tiled=True)]
    reduce_scatter x1 -> x0, waiting for transfers between devices: 41 us -> none  [per_device(): lax.psum_scatter(project_rows(picked, head), 'dp', scatter_dimension=0, t...]
    gather x4 -> x0, local copies, waits for them, and re-layouts: 20.4 us -> none  [the longest x1 16.9 us: per_device(): picked = jnp.take(every_row, place, axis=0)]
    dot_general x1 -> x0, matrix products: 20.4 us -> none  [project_rows(): lax.dot_general(rows, head, (((1,), (1,)), ((), ())), preferred_element_t...]
    all_to_all x1 -> x0, blocking collectives: 14.7 us -> none  [per_device(): lax.all_to_all(hidden, 'dp', split_axis=1, concat_axis=0, tiled=True)]
  transfers between devices with their start and end apart: 2 -> 0, of which waited for: 2 -> 0; matrix products, arithmetic and copies ran while one was open for 4% -> 0% of each run, Pallas kernels for 0% -> 0%
where the time goes in v1:
time: 123 us
  Pallas kernels  113 us (92%)
  local copies, waits for them, and re-layouts  8.02 us (7%)
  other arithmetic  1.25 us (1%)
    pallas_call x1, Pallas kernels, call(): pl.pallas_call(functools.partial(kernel, steps, by_arrival), out_shape=(j...  113 us
    unnamed x2, local copies, waits for them, and re-layouts  4.16 us

profile of v1, /device:TPU:0, one launch (start us, length us, event | category | flops | bytes accessed | tf_op | source)
XLA Modules:
  0.0 122.8 jit_solution(12119977705797427276)
XLA Ops:
  0.6 1.2 %broadcast_in_dim.10.blp = f32[1,288]{1,0:T(1,128)} reshape(f32[288]{0:T(512)} %param.13) | data formatting | bytes 2304 | tf_op jit(solution)/shard_map/broadcast_in_dim | solution.py:482
  1.9 1.3 %broadcast_in_dim.11.tlen = s32[1,288]{1,0:T(1,128)} reshape(s32[288]{0:T(512)} %param.14) | data formatting | bytes 2304 | tf_op jit(solution)/shard_map/broadcast_in_dim | solution.py:482
  3.1 1.4 %reshape.7.order = s32[4,192]{1,0:T(4,128)} reshape(s32[768]{0:T(1024)} %param.12) | data formatting | bytes 6144 | tf_op jit(solution)/shard_map/reshape | solution.py:481
  4.5 1.5 %copy.10.div = s32[192,16]{1,0:T(8,128)} copy(s32[192,16]{0,1:T(8,128)} %param.15) | data formatting | bytes 24576 | tf_op args[7]
  5.9 112.9 %shard_map.95 = (f32[192,2048]{1,0:T(8,128)}, f32[1,288]{1,0:T(1,128)}) custom-call(bf16[9,16384]{1,0:T(8,128)(2,1)} %hidden.1, bf16[2048,4096]{1,0:T(8,128)(2,1)} %head.1, f32[1,2048]{1,0:T(1,128)} %bitcast.1, s32[4]{0:T(128)} %live.1, s32[4,192]{1,0:T(4,128)} %reshape.7.order, f32[1,288]{1,0:T(1,128)} %broadcast_in_dim.10.blp, ...), custom_call_target="tpu_custom_call" | custom-call | tf_op jit(solution)/shard_map/pallas_call | solution.py:448
  118.9 1.2 %reduce = f32[288]{0:T(512)} reduce(f32[1,288]{1,0:T(1,128)} %get-tuple-element.5, f32[]{:T(128)} %constant.1), dimensions={0}, to_apply=%get-tuple-element.5.reduce_sub_computation | reduce | bytes 2308 | tf_op jit(solution)/shard_map/pallas_call | solution.py:448
  120.1 2.7 %copy.12 = f32[192,2048]{1,0:T(8,128)} copy(f32[192,2048]{1,0:T(8,128)} %get-tuple-element.8) | data formatting | bytes 3145728

commit v2 on v0

v2 whole, which is shorter than its diff:
```python
import functools

import jax
import jax.numpy as jnp
from jax import lax
from jax.experimental import pallas as pl
from jax.experimental.pallas import tpu as pltpu
from jax.sharding import PartitionSpec as P

F32, BF16, I32, I16 = jnp.float32, jnp.bfloat16, jnp.int32, jnp.int16
MESH = pl.DeviceIdType.MESH

PARTS = ((0, 1024), (1024, 1024), (2048, 1024), (3072, 512), (3584, 512))
CAP = 32
RB = 64
PIECE = 512


def iota(shape, axis):
    return lax.broadcasted_iota(I32, shape, axis)


def to_col(row, n, shift=0):
    width = row.shape[1]
    hit = iota((n, width), 0) + shift == iota((n, width), 1)
    return jnp.sum(jnp.where(hit, row, jnp.zeros_like(row)), axis=1, keepdims=True)


def to_row(col, width, shift=0):
    n = col.shape[0]
    hit = iota((n, width), 0) + shift == iota((n, width), 1)
    return jnp.sum(jnp.where(hit, col, jnp.zeros_like(col)), axis=0, keepdims=True)


def live_of_lane(count, lane):
    return (count - lane + 31) >> 5


def row_info(order, live):
    e0 = live[0]
    e1 = e0 + live[1]
    e2 = e1 + live[2]
    past = [(order >= e).astype(I32) for e in (e0, e1, e2)]
    replica = past[0] + past[1] + past[2]
    within = order - (past[0] * live[0] + past[1] * live[1] + past[2] * live[2])
    lane, depth = within & 31, within >> 5
    row = depth
    for i in range(3):
        row = row + past[i] * live_of_lane(live[i], lane)
    return replica, lane, depth, row


def place(lane, x, y):
    lx, ly, lc = lane >> 3, (lane >> 1) & 3, lane & 1
    dx, dy = (lx - x) & 3, (ly - y) & 3
    r1 = dx + lc * (dy - dx)
    r2 = dy + lc * (dx - dy)
    return (r2 ^ (r2 >> 1)) * 8 + lc * 4 + (r1 ^ (r1 >> 1))


def quantize(val):
    top = jnp.maximum(jnp.max(jnp.abs(val), axis=1, keepdims=True), 1e-30)
    coded = jnp.round(val * (32767.0 / top)).astype(I32).astype(I16)
    return coded, top * (1.0 / 32767.0)


def widen(coded):
    return coded.astype(I32).astype(F32)


def kernel(hidden, head, row_scale, live, order, blp, tlen, div,
           scored, slotn,
           hrecv, pool, headv, st, sel, xsel, S, CN,
           SP, SM, RM, RP, SP2, SM2, RM2, RP2,
           CP, CM, KM, KP, CP2, CM2, KM2, KP2,
           TA, TB, LS,
           head_sem, own_sem, out_sem, z_s, z_r, t_s, t_r,
           r1_s, r1_r, r2_s, r2_r, sib_s, sib_r,
           rs_s, rs_r, rt_s, rt_r, ta_s, ta_r, tb_s, tb_r, ls_s, ls_r):
    q = lax.axis_index("dp")
    v = lax.axis_index("vocab")
    x, y, c = v // 8, (v // 2) % 4, v % 2
    width = hidden.shape[1] // 4
    voc = head.shape[0]
    half_v = voc // 2
    rows_g = div.shape[1]
    slots = blp.shape[0]
    n_parts = len(PARTS)

    def dev(zz, xx, yy, cc):
        return (zz % 4, (xx % 4) * 8 + (yy % 4) * 2 + (cc % 2))

    zdev = [dev(q + d, x, y, c) for d in range(4)]
    fan = [(dy, dc) for dy in range(4) for dc in range(2)]
    adev = [dev(q, x, y + dy, c + dc) for dy, dc in fan]
    bdev = [dev(q, x + d, y, c) for d in range(4)]
    sibling = adev[1]
    r1p = dev(q, x + (1 - c), y + c, c)
    r1m = dev(q, x + 3 * (1 - c), y + 3 * c, c)
    r2p = dev(q, x + c, y + (1 - c), c)
    r2m = dev(q, x + 3 * c, y + 3 * (1 - c), c)
    sends = []

    def rc(src, dst, ss, rs, device):
        return pltpu.make_async_remote_copy(
            src_ref=src, dst_ref=dst, send_sem=ss, recv_sem=rs, device_id=device, device_id_type=MESH)

    def push(src, dst, ss, rs, device):
        copy = rc(src, dst, ss, rs, device)
        copy.start()
        sends.append(copy)

    def got(dst, rs):
        rc(dst, dst, t_s.at[0], rs, zdev[1]).wait_recv()

    barrier = pltpu.get_barrier_semaphore()
    peers = zdev[1:] + adev[1:] + bdev[1:]
    for device in peers:
        pl.semaphore_signal(barrier, inc=1, device_id=device, device_id_type=MESH)

    def part(k):
        return pl.ds(PARTS[k][0], PARTS[k][1])

    def quarter(group, k):
        at = pl.multiple_of(group * width + PARTS[k][0], 128)
        return hidden.at[:, pl.ds(at, PARTS[k][1])]

    own_copies = [pltpu.make_async_copy(quarter(q, k), hrecv.at[q, :, part(k)], own_sem.at[k]) for k in range(n_parts)]
    head_copies = [pltpu.make_async_copy(head.at[:, part(k)], headv.at[:, part(k)], head_sem.at[k])
                   for k in range(n_parts)]
    for copy in own_copies + head_copies:
        copy.start()
    st[q] = jnp.zeros(st.shape[1:], F32)
    st[q, 0:1, 0:slots] = blp[...].reshape(1, slots)
    lengths = tlen[...].reshape(1, slots).astype(F32)
    st[q, 1:2, 0:slots] = jnp.exp(0.8 * jnp.log((5.0 + lengths) / 6.0))
    for ref in (CP, CM, CP2, CM2):
        ref[...] = jnp.zeros(ref.shape, F32)
    TA[0] = jnp.zeros(TA.shape[1:], F32)
    TB[0] = jnp.zeros(TB.shape[1:], F32)
    LS[q] = jnp.zeros(LS.shape[1:], F32)

    pl.semaphore_wait(barrier, len(peers))

    for k in range(n_parts):
        for d in (2, 1, 3):
            push(quarter((q + d) % 4, k), hrecv.at[q, :, part(k)], z_s.at[k, d - 1], z_r.at[k, d - 1], zdev[d])
    for d in (1, 2, 3):
        push(st.at[q], st.at[q], t_s.at[d - 1], t_r.at[d - 1], zdev[d])

    numbers = order[...].reshape(1, 4 * rows_g)
    by_group = [numbers[:, g * rows_g:(g + 1) * rows_g] for g in range(4)]

    def order_of(group):
        return sum(jnp.where(group == g, by_group[g], 0) for g in range(4))

    for gi, group in enumerate(((q + 2) % 4, (q + 1) % 4, (q + 3) % 4, q)):
        _, lane, _, row = row_info(order_of(group), live)
        at = to_col(place(lane, x, y) * CAP + row, rows_g)
        for b in range(32 * CAP // 128):
            hit = at == iota((rows_g, 128), 1) + 128 * b
            sel[gi * rows_g:(gi + 1) * rows_g, b * 128:(b + 1) * 128] = jnp.where(hit, 1.0, 0.0).astype(BF16)

    counts = [live_of_lane(live[r], v) for r in range(4)]
    picks = []
    first = 0
    for r in range(4):
        i, j = iota((CAP, 9), 0), iota((CAP, 9), 1)
        picks.append(jnp.where((i == first + j) & (j < counts[r]), 1.0, 0.0).astype(BF16))
        first = first + counts[r]

    t4 = 4 * c
    u4 = 4 - t4

    def blk(idx, k, n=1):
        return pool.at[pl.ds(pl.multiple_of(idx * CAP, CAP), n * CAP), part(k)]

    def half(idx, h, k):
        return pool.at[pl.ds(pl.multiple_of(idx * CAP + h * (CAP // 2), CAP // 2), CAP // 2), part(k)]

    def to_sibling(r2, k):
        push(blk(r2 * 8 + t4, k, 4), blk(r2 * 8 + t4, k, 4), sib_s.at[k, r2], sib_r.at[k, r2], sibling)

    def stage1(k):
        own_copies[k].wait()
        for d in (1, 3, 2):
            got(hrecv.at[(q + 4 - d) % 4, :, part(k)], z_r.at[k, d - 1])
        acc = jnp.zeros((CAP, PARTS[k][1]), F32)
        for r in range(4):
            acc += jnp.dot(picks[r], hrecv[r, :, part(k)], preferred_element_type=F32)
        pool[pl.ds(pl.multiple_of(t4 * CAP, CAP), CAP), part(k)] = acc.astype(BF16)
        push(blk(t4, k), blk(t4 + 2, k), r1_s.at[k, 1], r1_r.at[k, 1], r1p)
        push(blk(t4, k), blk(t4 + 1, k), r1_s.at[k, 0], r1_r.at[k, 0], r1m)

    def stage2(k):
        got(blk(t4 + 1, k), r1_r.at[k, 0])
        push(half(t4 + 1, 0, k), half(t4 + 3, 0, k), r1_s.at[k, 2], r1_r.at[k, 2], r1m)
        got(blk(t4 + 2, k), r1_r.at[k, 1])
        push(half(t4 + 2, 1, k), half(t4 + 3, 1, k), r1_s.at[k, 3], r1_r.at[k, 3], r1p)

    def stage3(k):
        got(half(t4 + 3, 0, k), r1_r.at[k, 2])
        got(half(t4 + 3, 1, k), r1_r.at[k, 3])
        push(blk(t4, k, 4), blk(16 + t4, k, 4), r2_s.at[k, 1], r2_r.at[k, 1], r2p)
        push(blk(t4, k, 4), blk(8 + t4, k, 4), r2_s.at[k, 0], r2_r.at[k, 0], r2m)
        to_sibling(0, k)

    def stage4(k):
        got(blk(8 + t4, k, 4), r2_r.at[k, 0])
        push(blk(8 + t4, k, 2), blk(24 + t4, k, 2), r2_s.at[k, 2], r2_r.at[k, 2], r2m)
        got(blk(16 + t4, k, 4), r2_r.at[k, 1])
        push(blk(18 + t4, k, 2), blk(26 + t4, k, 2), r2_s.at[k, 3], r2_r.at[k, 3], r2p)
        to_sibling(1, k)
        to_sibling(2, k)

    def stage5(k):
        got(blk(24 + t4, k, 2), r2_r.at[k, 2])
        got(blk(26 + t4, k, 2), r2_r.at[k, 3])
        to_sibling(3, k)

    def select(k):
        for r2 in range(4):
            got(blk(r2 * 8 + u4, k, 4), sib_r.at[k, r2])
        start, size = PARTS[k]

        @pl.loop(0, size // 512)
        def _(n):
            off = pl.multiple_of(n * 512, 512)
            xsel[:, pl.ds(off, 512)] = jnp.dot(
                sel[...], pool[:, pl.ds(start + off, 512)], preferred_element_type=F32).astype(BF16)

    def multiply(k, lo, hi):
        start, size = PARTS[k]

        @pl.loop(lo // 256, hi // 256)
        def _(n):
            cols = pl.ds(pl.multiple_of(n * 256, 256), 256)
            out = lax.dot_general(xsel[:, 0:size], headv[cols, part(k)], (((1,), (1,)), ((), ())),
                                  preferred_element_type=F32)
            S[:, cols] = out if k == 0 else S[:, cols] + out

    def blocks(body):
        @pl.loop(0, rows_g // RB)
        def _(b):
            body(pl.multiple_of(b * RB, RB))

    def mine(gi, rows):
        return pl.ds(pl.multiple_of(gi * rows_g + rows, RB), RB)

    def cols_of(p):
        return slice(p * PIECE, (p + 1) * PIECE)

    def send_first(p):
        plus, minus = (0, 2) if p < 2 else (1, 0)

        def body(rows):
            r = pl.ds(rows, RB)
            for buf, scales, gi in ((SP, CP, plus), (SM, CM, minus)):
                coded, scale = quantize(S[mine(gi, rows), cols_of(p)])
                buf[r, cols_of(p)] = coded
                scales[p] += to_row(scale, 256, rows)

        blocks(body)
        push(SP.at[:, cols_of(p)], RM.at[:, cols_of(p)], rs_s.at[p, 0], rs_r.at[p, 0], zdev[1])
        push(SM.at[:, cols_of(p)], RP.at[:, cols_of(p)], rs_s.at[p, 1], rs_r.at[p, 1], zdev[3])
        push(CP.at[p], KM.at[p], rs_s.at[p, 2], rs_r.at[p, 2], zdev[1])
        push(CM.at[p], KP.at[p], rs_s.at[p, 3], rs_r.at[p, 3], zdev[3])

    def send_second(j):
        for p in (j, j + 2):
            got(RM.at[:, cols_of(p)], rs_r.at[p, 0])
            got(RP.at[:, cols_of(p)], rs_r.at[p, 1])
            got(KM.at[p], rs_r.at[p, 2])
            got(KP.at[p], rs_r.at[p, 3])

        def body(rows):
            r = pl.ds(rows, RB)
            for buf, scales, recv, rscale, gi, p in ((SP2, CP2, RM, KM, 1, j), (SM2, CM2, RP, KP, 2, j + 2)):
                old = widen(recv[r, cols_of(p)]) * to_col(rscale[p], RB, rows)
                coded, scale = quantize(S[mine(gi, rows), cols_of(p)] + old)
                buf[r, cols_of(j)] = coded
                scales[j] += to_row(scale, 256, rows)

        blocks(body)
        push(SP2.at[:, cols_of(j)], RM2.at[:, cols_of(j)], rt_s.at[j, 0], rt_r.at[j, 0], zdev[1])
        push(SM2.at[:, cols_of(j)], RP2.at[:, cols_of(j)], rt_s.at[j, 1], rt_r.at[j, 1], zdev[3])
        push(CP2.at[j], KM2.at[j], rt_s.at[j, 2], rt_r.at[j, 2], zdev[1])
        push(CM2.at[j], KP2.at[j], rt_s.at[j, 3], rt_r.at[j, 3], zdev[3])

    def finish(j):
        got(RM2.at[:, cols_of(j)], rt_r.at[j, 0])
        got(RP2.at[:, cols_of(j)], rt_r.at[j, 1])
        got(KM2.at[j], rt_r.at[j, 2])
        got(KP2.at[j], rt_r.at[j, 3])

        def body(rows):
            r = pl.ds(rows, RB)
            for p, near, nscale, far, fscale in ((j, RP, KP, RM2, KM2), (j + 2, RM, KM, RP2, KP2)):
                total = S[mine(3, rows), cols_of(p)]
                total += widen(near[r, cols_of(p)]) * to_col(nscale[p], RB, rows)
                total += widen(far[r, cols_of(j)]) * to_col(fscale[j], RB, rows)
                logits = total * row_scale[:, cols_of(p)]
                S[mine(3, rows), cols_of(p)] = logits
                top = jnp.max(logits, axis=1, keepdims=True)
                TA[0, p:p + 1, :] += to_row(top, 256, rows)
                TA[0, p + 4:p + 5, :] += to_row(jnp.sum(jnp.exp(logits - top), axis=1, keepdims=True), 256, rows)

        blocks(body)

    for i in range(n_parts + 2):
        if i < n_parts:
            stage1(i)
        if 0 <= i - 1 < n_parts:
            stage2(i - 1)
        if 0 <= i - 2:
            stage3(i - 2)
    stage4(0)
    stage4(1)
    for k in range(n_parts):
        stage5(k)
        select(k)
        if k + 2 < n_parts:
            stage4(k + 2)
        head_copies[k].wait()
        if k + 1 < n_parts:
            multiply(k, 0, voc)
    for p in (0, 2, 1, 3):
        multiply(n_parts - 1, p * PIECE, (p + 1) * PIECE)
        send_first(p)
    send_second(0)

    base = v * voc

    @pl.loop(0, rows_g // 32)
    def _(b):
        rows = pl.multiple_of(b * 32, 32)
        ids = [to_col(div[j:j + 1, :], 32, rows) - base for j in range(16)]
        for k in range(voc // 256):
            token = iota((32, 256), 1) + k * 256
            acc = jnp.zeros((32, 256), F32)
            for j in range(16):
                acc = acc - jnp.where(ids[j] == token, 0.5, 0.0)
            CN[pl.ds(rows, 32), k * 256:(k + 1) * 256] = acc

    send_second(1)

    for d in (1, 2, 3):
        got(st.at[(q + 4 - d) % 4], t_r.at[d - 1])
    replica, lane, depth, _ = row_info(order_of(q), live)
    slot_col = to_col(replica * slots + lane * 9 + depth, rows_g)
    score = jnp.zeros((rows_g, 1), F32)
    factor = jnp.zeros((rows_g, 1), F32)
    for r in range(4):
        hit = slot_col - r * slots == iota((rows_g, st.shape[2]), 1)
        score += jnp.sum(jnp.where(hit, st[r, 0:1, :], 0.0), axis=1, keepdims=True)
        factor += jnp.sum(jnp.where(hit, st[r, 1:2, :], 0.0), axis=1, keepdims=True)
    inverse = 1.0 / factor

    finish(0)
    finish(1)

    for i in range(1, 8):
        push(TA.at[0], TA.at[i], ta_s.at[i], ta_r.at[i], adev[i])

    def combine(tops, totals):
        top = functools.reduce(jnp.maximum, tops)
        return top, sum(total * jnp.exp(t - top) for t, total in zip(tops, totals))

    for i in range(1, 8):
        got(TA.at[i], ta_r.at[i])
    top, total = combine([TA[i, p:p + 1, :] for i in range(8) for p in range(4)],
                         [TA[i, p + 4:p + 5, :] for i in range(8) for p in range(4)])
    TB[0, 0:1, :] = top
    TB[0, 1:2, :] = total
    for i in range(1, 4):
        push(TB.at[0], TB.at[i], tb_s.at[i], tb_r.at[i], bdev[i])
    for i in range(1, 4):
        got(TB.at[i], tb_r.at[i])
    top, total = combine([TB[i, 0:1, :] for i in range(4)], [TB[i, 1:2, :] for i in range(4)])
    lse = to_col(top + jnp.log(total), rows_g)
    LS[q, 0:1, :] = to_row(lse, 256)
    for d in (1, 2, 3):
        push(LS.at[q], LS.at[q], ls_s.at[d - 1], ls_r.at[d - 1], zdev[d])
    shift = score - lse
    outs = []
    for p in range(voc // PIECE):
        CN[:, cols_of(p)] = (S[3 * rows_g:4 * rows_g, cols_of(p)] + CN[:, cols_of(p)] + shift) * inverse
        copy = pltpu.make_async_copy(CN.at[:, cols_of(p)], scored.at[:, cols_of(p)], out_sem.at[p])
        copy.start()
        outs.append(copy)

    for d in (1, 2, 3):
        got(LS.at[(q + 4 - d) % 4], ls_r.at[d - 1])
    acc = jnp.zeros((1, st.shape[2]), F32)
    for g in range(4):
        replica, lane, depth, _ = row_info(by_group[g], live)
        slot_col = to_col(replica * slots + lane * 9 + depth, rows_g)
        hit = slot_col - q * slots == iota((rows_g, st.shape[2]), 1)
        acc += jnp.sum(jnp.where(hit, to_col(LS[g, 0:1, :], rows_g), 0.0), axis=0, keepdims=True)
    slotn[...] = acc[:, 0:slots].reshape(slots)

    for copy in outs:
        copy.wait()
    for copy in sends:
        copy.wait_send()


def call(hidden, head, row_scale, live, order, blp, tlen, div):
    rows_g, voc, width, slots = div.shape[1], head.shape[0], head.shape[1], blp.shape[0]
    half_v = voc // 2
    n = len(PARTS)
    pieces = voc // PIECE
    dma = pltpu.SemaphoreType.DMA
    vmem = pl.BlockSpec(memory_space=pltpu.VMEM)
    anyspace = pl.BlockSpec(memory_space=pl.ANY)
    smem = pl.BlockSpec(memory_space=pltpu.SMEM)
    return pl.pallas_call(
        kernel,
        out_shape=(jax.ShapeDtypeStruct((rows_g, voc), F32), jax.ShapeDtypeStruct((slots,), F32)),
        in_specs=[anyspace, anyspace, vmem, smem, vmem, vmem, vmem, vmem],
        out_specs=(anyspace, vmem),
        scratch_shapes=[
            pltpu.VMEM((4, hidden.shape[0], width), BF16),
            pltpu.VMEM((32 * CAP, width), BF16),
            pltpu.VMEM((voc, width), BF16),
            pltpu.VMEM((4, 8, 384), F32),
            pltpu.VMEM((4 * rows_g, 32 * CAP), BF16),
            pltpu.VMEM((4 * rows_g, max(size for _, size in PARTS)), BF16),
            pltpu.VMEM((4 * rows_g, voc), F32),
            pltpu.VMEM((rows_g, voc), F32),
            *[pltpu.VMEM((rows_g, voc), I16)] * 4,
            *[pltpu.VMEM((rows_g, half_v), I16)] * 4,
            *[pltpu.VMEM((pieces, 1, 256), F32)] * 4,
            *[pltpu.VMEM((pieces // 2, 1, 256), F32)] * 4,
            pltpu.VMEM((8, 8, 256), F32),
            pltpu.VMEM((4, 8, 256), F32),
            pltpu.VMEM((4, 8, 256), F32),
            dma((n,)), dma((n,)), dma((pieces,)),
            dma((n, 3)), dma((n, 3)), dma((3,)), dma((3,)),
            dma((n, 4)), dma((n, 4)), dma((n, 4)), dma((n, 4)), dma((n, 4)), dma((n, 4)),
            dma((pieces, 4)), dma((pieces, 4)), dma((pieces // 2, 4)), dma((pieces // 2, 4)),
            dma((8,)), dma((8,)), dma((4,)), dma((4,)), dma((3,)), dma((3,)),
        ],
        compiler_params=pltpu.CompilerParams(
            collective_id=0, has_side_effects=True, vmem_limit_bytes=60 * 1024 * 1024),
    )(hidden, head, row_scale, live, order, blp, tlen, div)


def per_device(hidden, head, row_scale, live, order, beam_log_prob, token_length, div_ids):
    return call(hidden, head, row_scale[None, :], live, order, beam_log_prob, token_length, div_ids.T)


def solution(mesh):
    return jax.shard_map(
        per_device,
        mesh=mesh,
        in_specs=(
            P(("dp", "vocab"), None),
            P("vocab", "dp"),
            P("vocab"),
            P(),
            P(),
            P("dp"),
            P("dp"),
            P("dp", None),
        ),
        out_specs=(P("dp", "vocab"), P("dp")),
        check_vma=False,
    )
```

time: 350 us -> 115 us (0.33)
  blocking collectives: 165 us -> 0 us
  Pallas kernels: 0 us -> 111 us
  waiting for transfers between devices: 94.8 us -> 0 us
  local copies, waits for them, and re-layouts: 41.4 us -> 3.29 us
  matrix products: 20.4 us -> 0 us
  between operations: 14.9 us -> 0.65 us
  other arithmetic: 12 us -> 0 us
    pallas_call x0 -> x1, Pallas kernels: none -> 111 us  [call(): pl.pallas_call(kernel, out_shape=(jax.ShapeDtypeStruct((rows_g, voc), F32...]
    pmax x1 -> x0, blocking collectives: 67 us -> none  [per_device(): top = lax.pmax(local_top, 'vocab')]
    psum x1 -> x0, blocking collectives: 62.7 us -> none  [per_device(): total = lax.psum(jnp.sum(jnp.exp(logits - top[:, None]), axis=1), 'vocab')]
    all_gather x1 -> x0, waiting for transfers between devices: 53.8 us -> none  [per_device(): every_row = lax.all_gather(quarter, 'vocab', axis=0, tiled=True)]
    reduce_scatter x1 -> x0, waiting for transfers between devices: 41 us -> none  [per_device(): lax.psum_scatter(project_rows(picked, head), 'dp', scatter_dimension=0, t...]
    gather x4 -> x0, local copies, waits for them, and re-layouts: 20.4 us -> none  [the longest x1 16.9 us: per_device(): picked = jnp.take(every_row, place, axis=0)]
    dot_general x1 -> x0, matrix products: 20.4 us -> none  [project_rows(): lax.dot_general(rows, head, (((1,), (1,)), ((), ())), preferred_element_t...]
    all_to_all x1 -> x0, blocking collectives: 14.7 us -> none  [per_device(): lax.all_to_all(hidden, 'dp', split_axis=1, concat_axis=0, tiled=True)]
  transfers between devices with their start and end apart: 2 -> 0, of which waited for: 2 -> 0; matrix products, arithmetic and copies ran while one was open for 4% -> 0% of each run, Pallas kernels for 0% -> 0%
where the time goes in v2:
time: 115 us
  Pallas kernels  111 us (97%)
  local copies, waits for them, and re-layouts  3.29 us (3%)
    pallas_call x1, Pallas kernels, call(): pl.pallas_call(kernel, out_shape=(jax.ShapeDtypeStruct((rows_g, voc), F32...  111 us
    unnamed x4, local copies, waits for them, and re-layouts  3.29 us

profile of v2, /device:TPU:0, one launch (start us, length us, event | category | flops | bytes accessed | tf_op | source)
XLA Modules:
  0.0 115.1 jit_solution(1347317281288291176)
XLA Ops:
  0.6 111.1 %shard_map.95 = (f32[192,2048]{1,0:T(8,128)}, f32[288]{0:T(512)}) custom-call(bf16[9,16384]{1,0:T(8,128)(2,1)} %hidden.1, bf16[2048,4096]{1,0:T(8,128)(2,1)} %head.1, f32[1,2048]{1,0:T(1,128)} %bitcast.3, s32[4]{0:T(128)} %live.1, s32[768]{0:T(1024)} %order.1, f32[288]{0:T(512)} %blp.1, s32[288]{0:T(512)} %tlen.1, s32[16,192]{1,0:T(8,128)} %bitcast.2), custom_call_target="tpu_custom_call" | custom-call | tf_op jit(solution)/shard_map/pallas_call | solution.py:417
  111.8 0.0 copy-start
  111.8 2.7 %copy.12 = f32[192,2048]{1,0:T(8,128)} copy(f32[192,2048]{1,0:T(8,128)} %get-tuple-element.4) | data formatting | bytes 3145728
  114.5 0.0 copy-done
  114.5 0.6 copy.13
Async XLA Ops:
  111.8 2.7 %copy-start = (f32[288]{0:T(512)S(1)}, f32[288]{0:T(512)}, u32[]{:S(2)}) copy-start(f32[288]{0:T(512)} %get-tuple-element.5) | copy-start | bytes 3460

commit v3 on v2

--- a/solution.py
+++ b/solution.py
@@ -10,10 +10,9 @@
 F32, BF16, I32, I16 = jnp.float32, jnp.bfloat16, jnp.int32, jnp.int16
 MESH = pl.DeviceIdType.MESH
 
-PARTS = ((0, 1024), (1024, 1024), (2048, 1024), (3072, 512), (3584, 512))
 CAP = 32
-RB = 64
-PIECE = 512
+RB = 96
+PIECES = ((0, 256), (256, 256), (512, 512))
 
 
 def iota(shape, axis):
@@ -55,7 +54,11 @@
     dx, dy = (lx - x) & 3, (ly - y) & 3
     r1 = dx + lc * (dy - dx)
     r2 = dy + lc * (dx - dy)
-    return (r2 ^ (r2 >> 1)) * 8 + lc * 4 + (r1 ^ (r1 >> 1))
+    g1, g2 = r1 ^ (r1 >> 1), r2 ^ (r2 >> 1)
+    near = (g2 == 1) | (g2 == 2)
+    chunk = jnp.where(near, 1 + (g1 >> 1), g2)
+    minor = jnp.where(near, (g2 - 1) * 2 + (g1 & 1), g1)
+    return chunk * 8 + lc * 4 + minor
 
 
 def quantize(val):
@@ -73,7 +76,7 @@
            hrecv, pool, headv, st, sel, xsel, S, CN,
            SP, SM, RM, RP, SP2, SM2, RM2, RP2,
            CP, CM, KM, KP, CP2, CM2, KM2, KP2,
-           TA, TB, LS,
+           TL, TA, TB, LS,
            head_sem, own_sem, out_sem, z_s, z_r, t_s, t_r,
            r1_s, r1_r, r2_s, r2_r, sib_s, sib_r,
            rs_s, rs_r, rt_s, rt_r, ta_s, ta_r, tb_s, tb_r, ls_s, ls_r):
@@ -85,7 +88,7 @@
     half_v = voc // 2
     rows_g = div.shape[1]
     slots = blp.shape[0]
-    n_parts = len(PARTS)
+    n_pieces = len(PIECES)
 
     def dev(zz, xx, yy, cc):
         return (zz % 4, (xx % 4) * 8 + (yy % 4) * 2 + (cc % 2))
@@ -97,6 +100,7 @@
     sibling = adev[1]
     r1p = dev(q, x + (1 - c), y + c, c)
     r1m = dev(q, x + 3 * (1 - c), y + 3 * c, c)
+    r1f = dev(q, x + 2 * (1 - c), y + 2 * c, c)
     r2p = dev(q, x + c, y + (1 - c), c)
     r2m = dev(q, x + 3 * c, y + 3 * (1 - c), c)
     sends = []
@@ -118,33 +122,28 @@
     for device in peers:
         pl.semaphore_signal(barrier, inc=1, device_id=device, device_id_type=MESH)
 
-    def part(k):
-        return pl.ds(PARTS[k][0], PARTS[k][1])
-
-    def quarter(group, k):
-        at = pl.multiple_of(group * width + PARTS[k][0], 128)
-        return hidden.at[:, pl.ds(at, PARTS[k][1])]
-
-    own_copies = [pltpu.make_async_copy(quarter(q, k), hrecv.at[q, :, part(k)], own_sem.at[k]) for k in range(n_parts)]
-    head_copies = [pltpu.make_async_copy(head.at[:, part(k)], headv.at[:, part(k)], head_sem.at[k])
-                   for k in range(n_parts)]
-    for copy in own_copies + head_copies:
-        copy.start()
+    def quarter(group):
+        return hidden.at[:, pl.ds(pl.multiple_of(group * width, 128), width)]
+
+    own_copy = pltpu.make_async_copy(quarter(q), hrecv.at[q], own_sem)
+    own_copy.start()
+    head_copy = pltpu.make_async_copy(head, headv, head_sem)
+    head_copy.start()
     st[q] = jnp.zeros(st.shape[1:], F32)
     st[q, 0:1, 0:slots] = blp[...].reshape(1, slots)
     lengths = tlen[...].reshape(1, slots).astype(F32)
     st[q, 1:2, 0:slots] = jnp.exp(0.8 * jnp.log((5.0 + lengths) / 6.0))
     for ref in (CP, CM, CP2, CM2):
         ref[...] = jnp.zeros(ref.shape, F32)
+    TL[...] = jnp.zeros(TL.shape, F32)
     TA[0] = jnp.zeros(TA.shape[1:], F32)
     TB[0] = jnp.zeros(TB.shape[1:], F32)
     LS[q] = jnp.zeros(LS.shape[1:], F32)
 
     pl.semaphore_wait(barrier, len(peers))
 
-    for k in range(n_parts):
-        for d in (2, 1, 3):
-            push(quarter((q + d) % 4, k), hrecv.at[q, :, part(k)], z_s.at[k, d - 1], z_r.at[k, d - 1], zdev[d])
+    for d in (2, 1, 3):
+        push(quarter((q + d) % 4), hrecv.at[q], z_s.at[d - 1], z_r.at[d - 1], zdev[d])
     for d in (1, 2, 3):
         push(st.at[q], st.at[q], t_s.at[d - 1], t_r.at[d - 1], zdev[d])
 
@@ -172,72 +171,74 @@
     t4 = 4 * c
     u4 = 4 - t4
 
-    def blk(idx, k, n=1):
-        return pool.at[pl.ds(pl.multiple_of(idx * CAP, CAP), n * CAP), part(k)]
-
-    def half(idx, h, k):
-        return pool.at[pl.ds(pl.multiple_of(idx * CAP + h * (CAP // 2), CAP // 2), CAP // 2), part(k)]
-
-    def to_sibling(r2, k):
-        push(blk(r2 * 8 + t4, k, 4), blk(r2 * 8 + t4, k, 4), sib_s.at[k, r2], sib_r.at[k, r2], sibling)
-
-    def stage1(k):
-        own_copies[k].wait()
-        for d in (1, 3, 2):
-            got(hrecv.at[(q + 4 - d) % 4, :, part(k)], z_r.at[k, d - 1])
-        acc = jnp.zeros((CAP, PARTS[k][1]), F32)
+    def blk(idx):
+        return pool.at[pl.ds(pl.multiple_of(idx * CAP, CAP), CAP), :]
+
+    def half(idx, h):
+        return pool.at[pl.ds(pl.multiple_of(idx * CAP + h * (CAP // 2), CAP // 2), CAP // 2), :]
+
+    def to_sibling(ch, m):
+        push(blk(ch * 8 + t4 + m), blk(ch * 8 + t4 + m), sib_s.at[ch * 4 + m], sib_r.at[ch * 4 + m], sibling)
+
+    def from_sibling(ch):
+        for m in range(4):
+            got(blk(ch * 8 + u4 + m), sib_r.at[ch * 4 + m])
+
+    def spread(m):
+        ch, mm = 1 + (m >> 1), m & 1
+        push(blk(t4 + m), blk(ch * 8 + t4 + 2 + mm), r2_s.at[2 * m + 1], r2_r.at[2 * m + 1], r2p)
+        push(blk(t4 + m), blk(ch * 8 + t4 + mm), r2_s.at[2 * m], r2_r.at[2 * m], r2m)
+
+    own_copy.wait()
+    for d in (1, 3, 2):
+        got(hrecv.at[(q + 4 - d) % 4], z_r.at[d - 1])
+    for k in range(0, width, 1024):
+        acc = jnp.zeros((CAP, 1024), F32)
         for r in range(4):
-            acc += jnp.dot(picks[r], hrecv[r, :, part(k)], preferred_element_type=F32)
-        pool[pl.ds(pl.multiple_of(t4 * CAP, CAP), CAP), part(k)] = acc.astype(BF16)
-        push(blk(t4, k), blk(t4 + 2, k), r1_s.at[k, 1], r1_r.at[k, 1], r1p)
-        push(blk(t4, k), blk(t4 + 1, k), r1_s.at[k, 0], r1_r.at[k, 0], r1m)
-
-    def stage2(k):
-        got(blk(t4 + 1, k), r1_r.at[k, 0])
-        push(half(t4 + 1, 0, k), half(t4 + 3, 0, k), r1_s.at[k, 2], r1_r.at[k, 2], r1m)
-        got(blk(t4 + 2, k), r1_r.at[k, 1])
-        push(half(t4 + 2, 1, k), half(t4 + 3, 1, k), r1_s.at[k, 3], r1_r.at[k, 3], r1p)
-
-    def stage3(k):
-        got(half(t4 + 3, 0, k), r1_r.at[k, 2])
-        got(half(t4 + 3, 1, k), r1_r.at[k, 3])
-        push(blk(t4, k, 4), blk(16 + t4, k, 4), r2_s.at[k, 1], r2_r.at[k, 1], r2p)
-        push(blk(t4, k, 4), blk(8 + t4, k, 4), r2_s.at[k, 0], r2_r.at[k, 0], r2m)
-        to_sibling(0, k)
-
-    def stage4(k):
-        got(blk(8 + t4, k, 4), r2_r.at[k, 0])
-        push(blk(8 + t4, k, 2), blk(24 + t4, k, 2), r2_s.at[k, 2], r2_r.at[k, 2], r2m)
-        got(blk(16 + t4, k, 4), r2_r.at[k, 1])
-        push(blk(18 + t4, k, 2), blk(26 + t4, k, 2), r2_s.at[k, 3], r2_r.at[k, 3], r2p)
-        to_sibling(1, k)
-        to_sibling(2, k)
-
-    def stage5(k):
-        got(blk(24 + t4, k, 2), r2_r.at[k, 2])
-        got(blk(26 + t4, k, 2), r2_r.at[k, 3])
-        to_sibling(3, k)
-
-    def select(k):
-        for r2 in range(4):
-            got(blk(r2 * 8 + u4, k, 4), sib_r.at[k, r2])
-        start, size = PARTS[k]
-
-        @pl.loop(0, size // 512)
+            acc += jnp.dot(picks[r], hrecv[r, :, k:k + 1024], preferred_element_type=F32)
+        pool[pl.ds(pl.multiple_of(t4 * CAP, CAP), CAP), k:k + 1024] = acc.astype(BF16)
+
+    push(blk(t4), blk(t4 + 3), r1_s.at[2], r1_r.at[2], r1f)
+    push(blk(t4), blk(t4 + 2), r1_s.at[1], r1_r.at[1], r1p)
+    push(blk(t4), blk(t4 + 1), r1_s.at[0], r1_r.at[0], r1m)
+    to_sibling(0, 0)
+    spread(0)
+    for m in (1, 2, 3):
+        got(blk(t4 + m), r1_r.at[m - 1])
+        spread(m)
+        to_sibling(0, m)
+
+    def relay(ch):
+        for mm in range(2):
+            m = 2 * (ch - 1) + mm
+            got(blk(ch * 8 + t4 + mm), r2_r.at[2 * m])
+            push(half(ch * 8 + t4 + mm, 0), half(24 + t4 + m, 0), r2_s.at[8 + 2 * m], r2_r.at[8 + 2 * m], r2m)
+            got(blk(ch * 8 + t4 + 2 + mm), r2_r.at[2 * m + 1])
+            push(half(ch * 8 + t4 + 2 + mm, 1), half(24 + t4 + m, 1), r2_s.at[9 + 2 * m], r2_r.at[9 + 2 * m], r2p)
+            to_sibling(ch, mm)
+            to_sibling(ch, 2 + mm)
+
+    def relay_far():
+        for m in range(4):
+            got(half(24 + t4 + m, 0), r2_r.at[8 + 2 * m])
+            got(half(24 + t4 + m, 1), r2_r.at[9 + 2 * m])
+            to_sibling(3, m)
+
+    def select(lo, hi):
+        @pl.loop(0, width // 512)
         def _(n):
-            off = pl.multiple_of(n * 512, 512)
-            xsel[:, pl.ds(off, 512)] = jnp.dot(
-                sel[...], pool[:, pl.ds(start + off, 512)], preferred_element_type=F32).astype(BF16)
-
-    def multiply(k, lo, hi):
-        start, size = PARTS[k]
-
-        @pl.loop(lo // 256, hi // 256)
+            cols = pl.ds(pl.multiple_of(n * 512, 512), 512)
+            got_rows = jnp.dot(sel[:, lo * 256:hi * 256], pool[lo * 256:hi * 256, cols], preferred_element_type=F32)
+            xsel[:, cols] = (got_rows if lo == 0 else xsel[:, cols].astype(F32) + got_rows).astype(BF16)
+
+    def multiply(p):
+        start, size = piece(p)
+
+        @pl.loop(start // 256, (start + size) // 256)
         def _(n):
             cols = pl.ds(pl.multiple_of(n * 256, 256), 256)
-            out = lax.dot_general(xsel[:, 0:size], headv[cols, part(k)], (((1,), (1,)), ((), ())),
-                                  preferred_element_type=F32)
-            S[:, cols] = out if k == 0 else S[:, cols] + out
+            S[:, cols] = lax.dot_general(xsel[...], headv[cols, :], (((1,), (1,)), ((), ())),
+                                         preferred_element_type=F32)
 
     def blocks(body):
         @pl.loop(0, rows_g // RB)
@@ -245,13 +246,18 @@
             body(pl.multiple_of(b * RB, RB))
 
     def mine(gi, rows):
-        return pl.ds(pl.multiple_of(gi * rows_g + rows, RB), RB)
+        return pl.ds(pl.multiple_of(gi * rows_g + rows, 32), RB)
+
+    def piece(p):
+        start, size = PIECES[p % n_pieces]
+        return start + (p // n_pieces) * half_v, size
 
     def cols_of(p):
-        return slice(p * PIECE, (p + 1) * PIECE)
+        start, size = piece(p)
+        return slice(start, start + size)
 
     def send_first(p):
-        plus, minus = (0, 2) if p < 2 else (1, 0)
+        plus, minus = (0, 2) if p < n_pieces else (1, 0)
 
         def body(rows):
             r = pl.ds(rows, RB)
@@ -267,7 +273,7 @@
         push(CM.at[p], KP.at[p], rs_s.at[p, 3], rs_r.at[p, 3], zdev[3])
 
     def send_second(j):
-        for p in (j, j + 2):
+        for p in (j, j + n_pieces):
             got(RM.at[:, cols_of(p)], rs_r.at[p, 0])
             got(RP.at[:, cols_of(p)], rs_r.at[p, 1])
             got(KM.at[p], rs_r.at[p, 2])
@@ -275,7 +281,7 @@
 
         def body(rows):
             r = pl.ds(rows, RB)
-            for buf, scales, recv, rscale, gi, p in ((SP2, CP2, RM, KM, 1, j), (SM2, CM2, RP, KP, 2, j + 2)):
+            for buf, scales, recv, rscale, gi, p in ((SP2, CP2, RM, KM, 1, j), (SM2, CM2, RP, KP, 2, j + n_pieces)):
                 old = widen(recv[r, cols_of(p)]) * to_col(rscale[p], RB, rows)
                 coded, scale = quantize(S[mine(gi, rows), cols_of(p)] + old)
                 buf[r, cols_of(j)] = coded
@@ -295,39 +301,17 @@
 
         def body(rows):
             r = pl.ds(rows, RB)
-            for p, near, nscale, far, fscale in ((j, RP, KP, RM2, KM2), (j + 2, RM, KM, RP2, KP2)):
+            for p, near, nscale, far, fscale in ((j, RP, KP, RM2, KM2), (j + n_pieces, RM, KM, RP2, KP2)):
                 total = S[mine(3, rows), cols_of(p)]
                 total += widen(near[r, cols_of(p)]) * to_col(nscale[p], RB, rows)
                 total += widen(far[r, cols_of(j)]) * to_col(fscale[j], RB, rows)
                 logits = total * row_scale[:, cols_of(p)]
                 S[mine(3, rows), cols_of(p)] = logits
                 top = jnp.max(logits, axis=1, keepdims=True)
-                TA[0, p:p + 1, :] += to_row(top, 256, rows)
-                TA[0, p + 4:p + 5, :] += to_row(jnp.sum(jnp.exp(logits - top), axis=1, keepdims=True), 256, rows)
+                TL[p:p + 1, :] += to_row(top, 256, rows)
+                TL[p + 8:p + 9, :] += to_row(jnp.sum(jnp.exp(logits - top), axis=1, keepdims=True), 256, rows)
 
         blocks(body)
-
-    for i in range(n_parts + 2):
-        if i < n_parts:
-            stage1(i)
-        if 0 <= i - 1 < n_parts:
-            stage2(i - 1)
-        if 0 <= i - 2:
-            stage3(i - 2)
-    stage4(0)
-    stage4(1)
-    for k in range(n_parts):
-        stage5(k)
-        select(k)
-        if k + 2 < n_parts:
-            stage4(k + 2)
-        head_copies[k].wait()
-        if k + 1 < n_parts:
-            multiply(k, 0, voc)
-    for p in (0, 2, 1, 3):
-        multiply(n_parts - 1, p * PIECE, (p + 1) * PIECE)
-        send_first(p)
-    send_second(0)
 
     base = v * voc
 
@@ -342,7 +326,24 @@
                 acc = acc - jnp.where(ids[j] == token, 0.5, 0.0)
             CN[pl.ds(rows, 32), k * 256:(k + 1) * 256] = acc
 
-    send_second(1)
+    from_sibling(0)
+    relay(1)
+    from_sibling(1)
+    select(0, 2)
+    relay(2)
+    from_sibling(2)
+    select(2, 3)
+    relay_far()
+    from_sibling(3)
+    select(3, 4)
+    head_copy.wait()
+    for j in range(n_pieces):
+        for p in (j, j + n_pieces):
+            multiply(p)
+            send_first(p)
+        if j >= 1:
+            send_second(j - 1)
+    send_second(n_pieces - 1)
 
     for d in (1, 2, 3):
         got(st.at[(q + 4 - d) % 4], t_r.at[d - 1])
@@ -356,20 +357,21 @@
         factor += jnp.sum(jnp.where(hit, st[r, 1:2, :], 0.0), axis=1, keepdims=True)
     inverse = 1.0 / factor
 
-    finish(0)
-    finish(1)
-
-    for i in range(1, 8):
-        push(TA.at[0], TA.at[i], ta_s.at[i], ta_r.at[i], adev[i])
+    for j in range(n_pieces):
+        finish(j)
 
     def combine(tops, totals):
         top = functools.reduce(jnp.maximum, tops)
         return top, sum(total * jnp.exp(t - top) for t, total in zip(tops, totals))
 
+    top, total = combine([TL[p:p + 1, :] for p in range(2 * n_pieces)], [TL[p + 8:p + 9, :] for p in range(2 * n_pieces)])
+    TA[0, 0:1, :] = top
+    TA[0, 1:2, :] = total
+    for i in range(1, 8):
+        push(TA.at[0], TA.at[i], ta_s.at[i], ta_r.at[i], adev[i])
     for i in range(1, 8):
         got(TA.at[i], ta_r.at[i])
-    top, total = combine([TA[i, p:p + 1, :] for i in range(8) for p in range(4)],
-                         [TA[i, p + 4:p + 5, :] for i in range(8) for p in range(4)])
+    top, total = combine([TA[i, 0:1, :] for i in range(8)], [TA[i, 1:2, :] for i in range(8)])
     TB[0, 0:1, :] = top
     TB[0, 1:2, :] = total
     for i in range(1, 4):
@@ -383,7 +385,7 @@
         push(LS.at[q], LS.at[q], ls_s.at[d - 1], ls_r.at[d - 1], zdev[d])
     shift = score - lse
     outs = []
-    for p in range(voc // PIECE):
+    for p in range(2 * n_pieces):
         CN[:, cols_of(p)] = (S[3 * rows_g:4 * rows_g, cols_of(p)] + CN[:, cols_of(p)] + shift) * inverse
         copy = pltpu.make_async_copy(CN.at[:, cols_of(p)], scored.at[:, cols_of(p)], out_sem.at[p])
         copy.start()
@@ -408,8 +410,7 @@
 def call(hidden, head, row_scale, live, order, blp, tlen, div):
     rows_g, voc, width, slots = div.shape[1], head.shape[0], head.shape[1], blp.shape[0]
     half_v = voc // 2
-    n = len(PARTS)
-    pieces = voc // PIECE
+    n = 2 * len(PIECES)
     dma = pltpu.SemaphoreType.DMA
     vmem = pl.BlockSpec(memory_space=pltpu.VMEM)
     anyspace = pl.BlockSpec(memory_space=pl.ANY)
@@ -425,20 +426,21 @@
             pltpu.VMEM((voc, width), BF16),
             pltpu.VMEM((4, 8, 384), F32),
             pltpu.VMEM((4 * rows_g, 32 * CAP), BF16),
-            pltpu.VMEM((4 * rows_g, max(size for _, size in PARTS)), BF16),
+            pltpu.VMEM((4 * rows_g, width), BF16),
             pltpu.VMEM((4 * rows_g, voc), F32),
             pltpu.VMEM((rows_g, voc), F32),
             *[pltpu.VMEM((rows_g, voc), I16)] * 4,
             *[pltpu.VMEM((rows_g, half_v), I16)] * 4,
-            *[pltpu.VMEM((pieces, 1, 256), F32)] * 4,
-            *[pltpu.VMEM((pieces // 2, 1, 256), F32)] * 4,
+            *[pltpu.VMEM((n, 1, 256), F32)] * 4,
+            *[pltpu.VMEM((n // 2, 1, 256), F32)] * 4,
+            pltpu.VMEM((16, 256), F32),
             pltpu.VMEM((8, 8, 256), F32),
             pltpu.VMEM((4, 8, 256), F32),
             pltpu.VMEM((4, 8, 256), F32),
-            dma((n,)), dma((n,)), dma((pieces,)),
-            dma((n, 3)), dma((n, 3)), dma((3,)), dma((3,)),
-            dma((n, 4)), dma((n, 4)), dma((n, 4)), dma((n, 4)), dma((n, 4)), dma((n, 4)),
-            dma((pieces, 4)), dma((pieces, 4)), dma((pieces // 2, 4)), dma((pieces // 2, 4)),
+            dma, dma, dma((n,)),
+            dma((3,)), dma((3,)), dma((3,)), dma((3,)),
+            dma((3,)), dma((3,)), dma((16,)), dma((16,)), dma((16,)), dma((16,)),
+            dma((n, 4)), dma((n, 4)), dma((n // 2, 4)), dma((n // 2, 4)),
             dma((8,)), dma((8,)), dma((4,)), dma((4,)), dma((3,)), dma((3,)),
         ],
         compiler_params=pltpu.CompilerParams(

time: 115 us -> 106 us (0.922)
  Pallas kernels: 111 us -> 102 us
    pallas_call x1, Pallas kernels: 111 us -> 102 us  [call(): pl.pallas_call(kernel, out_shape=(jax.ShapeDtypeStruct((rows_g, voc), F32...]
where the time goes in v3:
time: 106 us; the launch traced here: 105 us
  Pallas kernels  102 us (96%)
  local copies, waits for them, and re-layouts  3.29 us (3%)
    pallas_call x1, Pallas kernels, call(): pl.pallas_call(kernel, out_shape=(jax.ShapeDtypeStruct((rows_g, voc), F32...  102 us
    unnamed x4, local copies, waits for them, and re-layouts  3.29 us

profile of v3, /device:TPU:0, one launch (start us, length us, event | category | flops | bytes accessed | tf_op | source)
XLA Modules:
  0.0 105.5 jit_solution(12925035475276177304)
XLA Ops:
  0.6 101.5 %shard_map.95 = (f32[192,2048]{1,0:T(8,128)}, f32[288]{0:T(512)}) custom-call(bf16[9,16384]{1,0:T(8,128)(2,1)} %hidden.1, bf16[2048,4096]{1,0:T(8,128)(2,1)} %head.1, f32[1,2048]{1,0:T(1,128)} %bitcast.3, s32[4]{0:T(128)} %live.1, s32[768]{0:T(1024)} %order.1, f32[288]{0:T(512)} %blp.1, s32[288]{0:T(512)} %tlen.1, s32[16,192]{1,0:T(8,128)} %bitcast.2), custom_call_target="tpu_custom_call" | custom-call | tf_op jit(solution)/shard_map/pallas_call | solution.py:418
  102.2 0.0 copy-start
  102.2 2.7 %copy.12 = f32[192,2048]{1,0:T(8,128)} copy(f32[192,2048]{1,0:T(8,128)} %get-tuple-element.4) | data formatting | bytes 3145728
  104.9 0.0 copy-done
  104.9 0.6 copy.13
Async XLA Ops:
  102.2 2.7 %copy-start = (f32[288]{0:T(512)S(1)}, f32[288]{0:T(512)}, u32[]{:S(2)}) copy-start(f32[288]{0:T(512)} %get-tuple-element.5) | copy-start | bytes 3460

commit v4 on v3

--- a/solution.py
+++ b/solution.py
@@ -12,7 +12,7 @@
 
 CAP = 32
 RB = 96
-PIECES = ((0, 256), (256, 256), (512, 512))
+PIECES = ((0, 256), (256, 512), (768, 256))
 
 
 def iota(shape, axis):
@@ -73,7 +73,7 @@
 
 def kernel(hidden, head, row_scale, live, order, blp, tlen, div,
            scored, slotn,
-           hrecv, pool, headv, st, sel, xsel, S, CN,
+           slotv, row8, fold, folded, pool, headv, st, sel, xsel, S, CN,
            SP, SM, RM, RP, SP2, SM2, RM2, RP2,
            CP, CM, KM, KP, CP2, CM2, KM2, KP2,
            TL, TA, TB, LS,
@@ -100,7 +100,6 @@
     sibling = adev[1]
     r1p = dev(q, x + (1 - c), y + c, c)
     r1m = dev(q, x + 3 * (1 - c), y + 3 * c, c)
-    r1f = dev(q, x + 2 * (1 - c), y + 2 * c, c)
     r2p = dev(q, x + c, y + (1 - c), c)
     r2m = dev(q, x + 3 * c, y + 3 * (1 - c), c)
     sends = []
@@ -122,10 +121,7 @@
     for device in peers:
         pl.semaphore_signal(barrier, inc=1, device_id=device, device_id_type=MESH)
 
-    def quarter(group):
-        return hidden.at[:, pl.ds(pl.multiple_of(group * width, 128), width)]
-
-    own_copy = pltpu.make_async_copy(quarter(q), hrecv.at[q], own_sem)
+    own_copy = pltpu.make_async_copy(hidden, slotv, own_sem)
     own_copy.start()
     head_copy = pltpu.make_async_copy(head, headv, head_sem)
     head_copy.start()
@@ -140,10 +136,25 @@
     TB[0] = jnp.zeros(TB.shape[1:], F32)
     LS[q] = jnp.zeros(LS.shape[1:], F32)
 
+    own_copy.wait()
+    run, hw = width // 16, width // 2
+    for g in range(4):
+        nine = slotv[:, g * width:(g + 1) * width].astype(F32)
+        fold[g * 16:(g + 1) * 16, 0:hw] = jnp.concatenate([nine[0:8, 0:hw], nine[0:8, hw:width]], axis=0).astype(BF16)
+        for i in range(16):
+            row8[i:i + 1, :] = nine[8:9, i * run:(i + 1) * run]
+        fold[g * 16:(g + 1) * 16, hw:hw + run] = row8[...].astype(BF16)
+
+    def rows16(ref, group):
+        return ref.at[pl.ds(pl.multiple_of(group * 16, 16), 16), :]
+
+    keep = pltpu.make_async_copy(rows16(fold, q), rows16(folded, q), own_sem)
+    keep.start()
+
     pl.semaphore_wait(barrier, len(peers))
 
     for d in (2, 1, 3):
-        push(quarter((q + d) % 4), hrecv.at[q], z_s.at[d - 1], z_r.at[d - 1], zdev[d])
+        push(rows16(fold, (q + d) % 4), rows16(folded, q), z_s.at[d - 1], z_r.at[d - 1], zdev[d])
     for d in (1, 2, 3):
         push(st.at[q], st.at[q], t_s.at[d - 1], t_r.at[d - 1], zdev[d])
 
@@ -160,13 +171,35 @@
             hit = at == iota((rows_g, 128), 1) + 128 * b
             sel[gi * rows_g:(gi + 1) * rows_g, b * 128:(b + 1) * 128] = jnp.where(hit, 1.0, 0.0).astype(BF16)
 
+    base = v * voc
+
+    @pl.loop(0, rows_g // 32)
+    def _(b):
+        rows = pl.multiple_of(b * 32, 32)
+        ids = [to_col(div[j:j + 1, :], 32, rows) - base for j in range(16)]
+        for k in range(voc // 256):
+            token = iota((32, 256), 1) + k * 256
+            acc = jnp.zeros((32, 256), F32)
+            for j in range(16):
+                acc = acc - jnp.where(ids[j] == token, 0.5, 0.0)
+            CN[pl.ds(rows, 32), k * 256:(k + 1) * 256] = acc
+
     counts = [live_of_lane(live[r], v) for r in range(4)]
-    picks = []
-    first = 0
-    for r in range(4):
-        i, j = iota((CAP, 9), 0), iota((CAP, 9), 1)
-        picks.append(jnp.where((i == first + j) & (j < counts[r]), 1.0, 0.0).astype(BF16))
-        first = first + counts[r]
+    firsts = [0]
+    for r in range(3):
+        firsts.append(firsts[-1] + counts[r])
+
+    def by_replica(values, r):
+        return sum(jnp.where(r == i, values[i], 0) for i in range(4))
+
+    i, j = iota((2 * CAP, 64), 0), iota((2 * CAP, 64), 1)
+    replica, depth = j >> 4, j & 7
+    hit = ((i >> 5) == ((j >> 3) & 1)) & ((i & 31) == by_replica(firsts, replica) + depth)
+    pick = jnp.where(hit & (depth < by_replica(counts, replica)), 1.0, 0.0).astype(BF16)
+    i, j = iota((16 * CAP, 64), 0), iota((16 * CAP, 64), 1)
+    replica = j >> 4
+    hit = ((i >> 5) == (j & 15)) & ((i & 31) == by_replica(firsts, replica) + 8)
+    pick8 = jnp.where(hit & (by_replica(counts, replica) > 8), 1.0, 0.0).astype(BF16)
 
     t4 = 4 * c
     u4 = 4 - t4
@@ -189,37 +222,47 @@
         push(blk(t4 + m), blk(ch * 8 + t4 + 2 + mm), r2_s.at[2 * m + 1], r2_r.at[2 * m + 1], r2p)
         push(blk(t4 + m), blk(ch * 8 + t4 + mm), r2_s.at[2 * m], r2_r.at[2 * m], r2m)
 
-    own_copy.wait()
+    keep.wait()
     for d in (1, 3, 2):
-        got(hrecv.at[(q + 4 - d) % 4], z_r.at[d - 1])
-    for k in range(0, width, 1024):
-        acc = jnp.zeros((CAP, 1024), F32)
-        for r in range(4):
-            acc += jnp.dot(picks[r], hrecv[r, :, k:k + 1024], preferred_element_type=F32)
-        pool[pl.ds(pl.multiple_of(t4 * CAP, CAP), CAP), k:k + 1024] = acc.astype(BF16)
-
-    push(blk(t4), blk(t4 + 3), r1_s.at[2], r1_r.at[2], r1f)
+        got(rows16(folded, (q + 4 - d) % 4), z_r.at[d - 1])
+    ninth = jnp.dot(pick8, folded[:, hw:hw + run], preferred_element_type=F32)
+    for k in range(0, hw, 1024):
+        both = jnp.dot(pick, folded[:, k:k + 1024], preferred_element_type=F32)
+        for h in range(2):
+            for n in range(0, 1024, run):
+                at = h * hw + k + n
+                b = at // run
+                block = both[h * CAP:(h + 1) * CAP, n:n + run] + ninth[b * CAP:(b + 1) * CAP, :]
+                pool[pl.ds(pl.multiple_of(t4 * CAP, CAP), CAP), at:at + run] = block.astype(BF16)
+
     push(blk(t4), blk(t4 + 2), r1_s.at[1], r1_r.at[1], r1p)
     push(blk(t4), blk(t4 + 1), r1_s.at[0], r1_r.at[0], r1m)
     to_sibling(0, 0)
     spread(0)
-    for m in (1, 2, 3):
-        got(blk(t4 + m), r1_r.at[m - 1])
-        spread(m)
-        to_sibling(0, m)
-
-    def relay(ch):
-        for mm in range(2):
-            m = 2 * (ch - 1) + mm
-            got(blk(ch * 8 + t4 + mm), r2_r.at[2 * m])
-            push(half(ch * 8 + t4 + mm, 0), half(24 + t4 + m, 0), r2_s.at[8 + 2 * m], r2_r.at[8 + 2 * m], r2m)
-            got(blk(ch * 8 + t4 + 2 + mm), r2_r.at[2 * m + 1])
-            push(half(ch * 8 + t4 + 2 + mm, 1), half(24 + t4 + m, 1), r2_s.at[9 + 2 * m], r2_r.at[9 + 2 * m], r2p)
-            to_sibling(ch, mm)
-            to_sibling(ch, 2 + mm)
-
-    def relay_far():
-        for m in range(4):
+    got(blk(t4 + 1), r1_r.at[0])
+    push(half(t4 + 1, 0), half(t4 + 3, 0), r1_s.at[2], r1_r.at[2], r1m)
+    got(blk(t4 + 2), r1_r.at[1])
+    push(half(t4 + 2, 1), half(t4 + 3, 1), r1_s.at[3], r1_r.at[3], r1p)
+    spread(1)
+    spread(2)
+    to_sibling(0, 1)
+    to_sibling(0, 2)
+    got(half(t4 + 3, 0), r1_r.at[2])
+    got(half(t4 + 3, 1), r1_r.at[3])
+    spread(3)
+    to_sibling(0, 3)
+
+    def relay(m):
+        ch, mm = 1 + (m >> 1), m & 1
+        got(blk(ch * 8 + t4 + mm), r2_r.at[2 * m])
+        push(half(ch * 8 + t4 + mm, 0), half(24 + t4 + m, 0), r2_s.at[8 + 2 * m], r2_r.at[8 + 2 * m], r2m)
+        got(blk(ch * 8 + t4 + 2 + mm), r2_r.at[2 * m + 1])
+        push(half(ch * 8 + t4 + 2 + mm, 1), half(24 + t4 + m, 1), r2_s.at[9 + 2 * m], r2_r.at[9 + 2 * m], r2p)
+        to_sibling(ch, mm)
+        to_sibling(ch, 2 + mm)
+
+    def relay_far(first):
+        for m in (first, first + 1):
             got(half(24 + t4 + m, 0), r2_r.at[8 + 2 * m])
             got(half(24 + t4 + m, 1), r2_r.at[9 + 2 * m])
             to_sibling(3, m)
@@ -231,14 +274,12 @@
             got_rows = jnp.dot(sel[:, lo * 256:hi * 256], pool[lo * 256:hi * 256, cols], preferred_element_type=F32)
             xsel[:, cols] = (got_rows if lo == 0 else xsel[:, cols].astype(F32) + got_rows).astype(BF16)
 
-    def multiply(p):
-        start, size = piece(p)
-
+    def multiply(start, size, lo, hi):
         @pl.loop(start // 256, (start + size) // 256)
         def _(n):
             cols = pl.ds(pl.multiple_of(n * 256, 256), 256)
-            S[:, cols] = lax.dot_general(xsel[...], headv[cols, :], (((1,), (1,)), ((), ())),
-                                         preferred_element_type=F32)
+            S[lo:hi, cols] = lax.dot_general(xsel[lo:hi, :], headv[cols, :], (((1,), (1,)), ((), ())),
+                                             preferred_element_type=F32)
 
     def blocks(body):
         @pl.loop(0, rows_g // RB)
@@ -313,37 +354,31 @@
 
         blocks(body)
 
-    base = v * voc
-
-    @pl.loop(0, rows_g // 32)
-    def _(b):
-        rows = pl.multiple_of(b * 32, 32)
-        ids = [to_col(div[j:j + 1, :], 32, rows) - base for j in range(16)]
-        for k in range(voc // 256):
-            token = iota((32, 256), 1) + k * 256
-            acc = jnp.zeros((32, 256), F32)
-            for j in range(16):
-                acc = acc - jnp.where(ids[j] == token, 0.5, 0.0)
-            CN[pl.ds(rows, 32), k * 256:(k + 1) * 256] = acc
-
+    relay(0)
     from_sibling(0)
+    select(0, 1)
     relay(1)
+    relay(2)
     from_sibling(1)
-    select(0, 2)
-    relay(2)
+    relay(3)
     from_sibling(2)
-    select(2, 3)
-    relay_far()
+    relay_far(0)
+    select(1, 3)
+    relay_far(2)
     from_sibling(3)
     select(3, 4)
     head_copy.wait()
+
+    others = 3 * rows_g
     for j in range(n_pieces):
         for p in (j, j + n_pieces):
-            multiply(p)
+            multiply(*piece(p), 0, others)
             send_first(p)
         if j >= 1:
             send_second(j - 1)
+    multiply(0, half_v, others, 4 * rows_g)
     send_second(n_pieces - 1)
+    multiply(half_v, half_v, others, 4 * rows_g)
 
     for d in (1, 2, 3):
         got(st.at[(q + 4 - d) % 4], t_r.at[d - 1])
@@ -421,7 +456,10 @@
         in_specs=[anyspace, anyspace, vmem, smem, vmem, vmem, vmem, vmem],
         out_specs=(anyspace, vmem),
         scratch_shapes=[
-            pltpu.VMEM((4, hidden.shape[0], width), BF16),
+            pltpu.VMEM(hidden.shape, BF16),
+            pltpu.VMEM((16, width // 16), F32),
+            pltpu.VMEM((64, width // 2 + width // 16), BF16),
+            pltpu.VMEM((64, width // 2 + width // 16), BF16),
             pltpu.VMEM((32 * CAP, width), BF16),
             pltpu.VMEM((voc, width), BF16),
             pltpu.VMEM((4, 8, 384), F32),
@@ -439,7 +477,7 @@
             pltpu.VMEM((4, 8, 256), F32),
             dma, dma, dma((n,)),
             dma((3,)), dma((3,)), dma((3,)), dma((3,)),
-            dma((3,)), dma((3,)), dma((16,)), dma((16,)), dma((16,)), dma((16,)),
+            dma((4,)), dma((4,)), dma((16,)), dma((16,)), dma((16,)), dma((16,)),
             dma((n, 4)), dma((n, 4)), dma((n // 2, 4)), dma((n // 2, 4)),
             dma((8,)), dma((8,)), dma((4,)), dma((4,)), dma((3,)), dma((3,)),
         ],

time: 106 us -> 96.1 us (0.907)
  Pallas kernels: 102 us -> 92 us
    pallas_call x1, Pallas kernels: 102 us -> 92 us  [call(): pl.pallas_call(kernel, out_shape=(jax.ShapeDtypeStruct((rows_g, voc), F32...]
where the time goes in v4:
time: 96.1 us; the launch traced here: 95.9 us
  Pallas kernels  92 us (96%)
  local copies, waits for them, and re-layouts  3.29 us (3%)
    pallas_call x1, Pallas kernels, call(): pl.pallas_call(kernel, out_shape=(jax.ShapeDtypeStruct((rows_g, voc), F32...  92 us
    unnamed x4, local copies, waits for them, and re-layouts  3.29 us

profile of v4, /device:TPU:0, one launch (start us, length us, event | category | flops | bytes accessed | tf_op | source)
XLA Modules:
  0.0 95.9 jit_solution(2316425167151992083)
XLA Ops:
  0.6 92.0 %shard_map.95 = (f32[192,2048]{1,0:T(8,128)}, f32[288]{0:T(512)}) custom-call(bf16[9,16384]{1,0:T(8,128)(2,1)} %hidden.1, bf16[2048,4096]{1,0:T(8,128)(2,1)} %head.1, f32[1,2048]{1,0:T(1,128)} %bitcast.3, s32[4]{0:T(128)} %live.1, s32[768]{0:T(1024)} %order.1, f32[288]{0:T(512)} %blp.1, s32[288]{0:T(512)} %tlen.1, s32[16,192]{1,0:T(8,128)} %bitcast.2), custom_call_target="tpu_custom_call" | custom-call | tf_op jit(solution)/shard_map/pallas_call | solution.py:453
  92.6 0.0 copy-start
  92.7 2.7 %copy.12 = f32[192,2048]{1,0:T(8,128)} copy(f32[192,2048]{1,0:T(8,128)} %get-tuple-element.4) | data formatting | bytes 3145728
  95.4 0.0 copy-done
  95.4 0.6 copy.13
Async XLA Ops:
  92.6 2.7 %copy-start = (f32[288]{0:T(512)S(1)}, f32[288]{0:T(512)}, u32[]{:S(2)}) copy-start(f32[288]{0:T(512)} %get-tuple-element.5) | copy-start | bytes 3460

commit v5 on v4

--- a/solution.py
+++ b/solution.py
@@ -11,7 +11,7 @@
 MESH = pl.DeviceIdType.MESH
 
 CAP = 32
-RB = 96
+RB = 192
 PIECES = ((0, 256), (256, 512), (768, 256))
 
 
@@ -71,13 +71,14 @@
     return coded.astype(I32).astype(F32)
 
 
-def kernel(hidden, head, row_scale, live, order, blp, tlen, div,
+def kernel(hidden, head, row_scale_in, live_in, order_in, blp_in, tlen_in, div_in,
            scored, slotn,
+           row_scale, live, order, blp, tlen, div,
            slotv, row8, fold, folded, pool, headv, st, sel, xsel, S, CN,
            SP, SM, RM, RP, SP2, SM2, RM2, RP2,
            CP, CM, KM, KP, CP2, CM2, KM2, KP2,
            TL, TA, TB, LS,
-           head_sem, own_sem, out_sem, z_s, z_r, t_s, t_r,
+           head_sem, own_sem, in_sem, out_sem, z_s, z_r, t_s, t_r,
            r1_s, r1_r, r2_s, r2_r, sib_s, sib_r,
            rs_s, rs_r, rt_s, rt_r, ta_s, ta_r, tb_s, tb_r, ls_s, ls_r):
     q = lax.axis_index("dp")
@@ -123,8 +124,14 @@
 
     own_copy = pltpu.make_async_copy(hidden, slotv, own_sem)
     own_copy.start()
+    small = [pltpu.make_async_copy(src, dst, in_sem.at[i]) for i, (src, dst) in enumerate((
+        (blp_in, blp), (tlen_in, tlen), (live_in, live), (order_in, order), (div_in, div), (row_scale_in, row_scale)))]
+    for copy in small:
+        copy.start()
     head_copy = pltpu.make_async_copy(head, headv, head_sem)
     head_copy.start()
+    for copy in small:
+        copy.wait()
     st[q] = jnp.zeros(st.shape[1:], F32)
     st[q, 0:1, 0:slots] = blp[...].reshape(1, slots)
     lengths = tlen[...].reshape(1, slots).astype(F32)
@@ -267,12 +274,12 @@
             got(half(24 + t4 + m, 1), r2_r.at[9 + 2 * m])
             to_sibling(3, m)
 
-    def select(lo, hi):
+    def select(lo, hi, top, end):
         @pl.loop(0, width // 512)
         def _(n):
             cols = pl.ds(pl.multiple_of(n * 512, 512), 512)
-            got_rows = jnp.dot(sel[:, lo * 256:hi * 256], pool[lo * 256:hi * 256, cols], preferred_element_type=F32)
-            xsel[:, cols] = (got_rows if lo == 0 else xsel[:, cols].astype(F32) + got_rows).astype(BF16)
+            found = jnp.dot(sel[top:end, lo * 256:hi * 256], pool[lo * 256:hi * 256, cols], preferred_element_type=F32)
+            xsel[top:end, cols] = (found if lo == 0 else xsel[top:end, cols].astype(F32) + found).astype(BF16)
 
     def multiply(start, size, lo, hi):
         @pl.loop(start // 256, (start + size) // 256)
@@ -354,31 +361,32 @@
 
         blocks(body)
 
+    others, every = 3 * rows_g, 4 * rows_g
     relay(0)
     from_sibling(0)
-    select(0, 1)
     relay(1)
     relay(2)
     from_sibling(1)
+    select(0, 2, 0, others)
     relay(3)
+    relay_far(0)
     from_sibling(2)
-    relay_far(0)
-    select(1, 3)
+    select(2, 3, 0, others)
     relay_far(2)
     from_sibling(3)
-    select(3, 4)
+    select(3, 4, 0, others)
     head_copy.wait()
 
-    others = 3 * rows_g
     for j in range(n_pieces):
         for p in (j, j + n_pieces):
             multiply(*piece(p), 0, others)
             send_first(p)
         if j >= 1:
             send_second(j - 1)
-    multiply(0, half_v, others, 4 * rows_g)
+    select(0, 4, others, every)
+    multiply(0, half_v, others, every)
     send_second(n_pieces - 1)
-    multiply(half_v, half_v, others, 4 * rows_g)
+    multiply(half_v, half_v, others, every)
 
     for d in (1, 2, 3):
         got(st.at[(q + 4 - d) % 4], t_r.at[d - 1])
@@ -449,13 +457,19 @@
     dma = pltpu.SemaphoreType.DMA
     vmem = pl.BlockSpec(memory_space=pltpu.VMEM)
     anyspace = pl.BlockSpec(memory_space=pl.ANY)
-    smem = pl.BlockSpec(memory_space=pltpu.SMEM)
+    hbm = pl.BlockSpec(memory_space=pltpu.HBM)
     return pl.pallas_call(
         kernel,
         out_shape=(jax.ShapeDtypeStruct((rows_g, voc), F32), jax.ShapeDtypeStruct((slots,), F32)),
-        in_specs=[anyspace, anyspace, vmem, smem, vmem, vmem, vmem, vmem],
+        in_specs=[hbm] * 8,
         out_specs=(anyspace, vmem),
         scratch_shapes=[
+            pltpu.VMEM(row_scale.shape, F32),
+            pltpu.SMEM(live.shape, I32),
+            pltpu.VMEM(order.shape, I32),
+            pltpu.VMEM(blp.shape, F32),
+            pltpu.VMEM(tlen.shape, I32),
+            pltpu.VMEM(div.shape, I32),
             pltpu.VMEM(hidden.shape, BF16),
             pltpu.VMEM((16, width // 16), F32),
             pltpu.VMEM((64, width // 2 + width // 16), BF16),
@@ -475,7 +489,7 @@
             pltpu.VMEM((8, 8, 256), F32),
             pltpu.VMEM((4, 8, 256), F32),
             pltpu.VMEM((4, 8, 256), F32),
-            dma, dma, dma((n,)),
+            dma, dma, dma((6,)), dma((n,)),
             dma((3,)), dma((3,)), dma((3,)), dma((3,)),
             dma((4,)), dma((4,)), dma((16,)), dma((16,)), dma((16,)), dma((16,)),
             dma((n, 4)), dma((n, 4)), dma((n // 2, 4)), dma((n // 2, 4)),

time: 96.1 us -> 92.7 us (0.965)
  Pallas kernels: 92 us -> 88.6 us
    pallas_call x1, Pallas kernels: 92 us -> 88.6 us  [call(): pl.pallas_call(kernel, out_shape=(jax.ShapeDtypeStruct((rows_g, voc), F32...]
where the time goes in v5:
time: 92.7 us; the launch traced here: 92.5 us
  Pallas kernels  88.6 us (96%)
  local copies, waits for them, and re-layouts  3.29 us (4%)
    pallas_call x1, Pallas kernels, call(): pl.pallas_call(kernel, out_shape=(jax.ShapeDtypeStruct((rows_g, voc), F32...  88.6 us
    unnamed x4, local copies, waits for them, and re-layouts  3.29 us

profile of v5, /device:TPU:0, one launch (start us, length us, event | category | flops | bytes accessed | tf_op | source)
XLA Modules:
  0.0 92.5 jit_solution(11451536125578447858)
XLA Ops:
  0.6 88.6 %shard_map.95 = (f32[192,2048]{1,0:T(8,128)}, f32[288]{0:T(512)}) custom-call(bf16[9,16384]{1,0:T(8,128)(2,1)} %hidden.1, bf16[2048,4096]{1,0:T(8,128)(2,1)} %head.1, f32[1,2048]{1,0:T(1,128)} %bitcast.3, s32[4]{0:T(128)} %live_in.1, s32[768]{0:T(1024)} %order_in.1, f32[288]{0:T(512)} %blp_in.1, s32[288]{0:T(512)} %tlen_in.1, s32[16,192]{1,0:T(8,128)} %bitcast.2), custom_call_target="tpu_custom_call" | custom-call | tf_op jit(solution)/shard_map/pallas_call | solution.py:461
  89.2 0.0 copy-start
  89.3 2.7 %copy.12 = f32[192,2048]{1,0:T(8,128)} copy(f32[192,2048]{1,0:T(8,128)} %get-tuple-element.4) | data formatting | bytes 3145728
  92.0 0.0 copy-done
  92.0 0.6 copy.13
Async XLA Ops:
  89.2 2.7 %copy-start = (f32[288]{0:T(512)S(1)}, f32[288]{0:T(512)}, u32[]{:S(2)}) copy-start(f32[288]{0:T(512)} %get-tuple-element.5) | copy-start | bytes 3460

commit v6 on v5

--- a/solution.py
+++ b/solution.py
@@ -118,7 +118,7 @@
         rc(dst, dst, t_s.at[0], rs, zdev[1]).wait_recv()
 
     barrier = pltpu.get_barrier_semaphore()
-    peers = zdev[1:] + adev[1:] + bdev[1:]
+    peers = [zdev[2], bdev[2], adev[5], adev[4], zdev[1], zdev[3], bdev[1], bdev[3]] + adev[1:4] + adev[6:]
     for device in peers:
         pl.semaphore_signal(barrier, inc=1, device_id=device, device_id_type=MESH)
 
@@ -307,18 +307,16 @@
     def send_first(p):
         plus, minus = (0, 2) if p < n_pieces else (1, 0)
 
-        def body(rows):
-            r = pl.ds(rows, RB)
-            for buf, scales, gi in ((SP, CP, plus), (SM, CM, minus)):
+        for buf, scales, gi, to, recv, side, device in (
+                (SP, CP, plus, RM, KM, 0, zdev[1]), (SM, CM, minus, RP, KP, 1, zdev[3])):
+            def body(rows):
                 coded, scale = quantize(S[mine(gi, rows), cols_of(p)])
-                buf[r, cols_of(p)] = coded
+                buf[pl.ds(rows, RB), cols_of(p)] = coded
                 scales[p] += to_row(scale, 256, rows)
 
-        blocks(body)
-        push(SP.at[:, cols_of(p)], RM.at[:, cols_of(p)], rs_s.at[p, 0], rs_r.at[p, 0], zdev[1])
-        push(SM.at[:, cols_of(p)], RP.at[:, cols_of(p)], rs_s.at[p, 1], rs_r.at[p, 1], zdev[3])
-        push(CP.at[p], KM.at[p], rs_s.at[p, 2], rs_r.at[p, 2], zdev[1])
-        push(CM.at[p], KP.at[p], rs_s.at[p, 3], rs_r.at[p, 3], zdev[3])
+            blocks(body)
+            push(buf.at[:, cols_of(p)], to.at[:, cols_of(p)], rs_s.at[p, side], rs_r.at[p, side], device)
+            push(scales.at[p], recv.at[p], rs_s.at[p, side + 2], rs_r.at[p, side + 2], device)
 
     def send_second(j):
         for p in (j, j + n_pieces):
@@ -410,23 +408,23 @@
     top, total = combine([TL[p:p + 1, :] for p in range(2 * n_pieces)], [TL[p + 8:p + 9, :] for p in range(2 * n_pieces)])
     TA[0, 0:1, :] = top
     TA[0, 1:2, :] = total
-    for i in range(1, 8):
+    for i in (5, 4, 3, 7, 2, 6, 1):
         push(TA.at[0], TA.at[i], ta_s.at[i], ta_r.at[i], adev[i])
     for i in range(1, 8):
         got(TA.at[i], ta_r.at[i])
     top, total = combine([TA[i, 0:1, :] for i in range(8)], [TA[i, 1:2, :] for i in range(8)])
     TB[0, 0:1, :] = top
     TB[0, 1:2, :] = total
-    for i in range(1, 4):
+    for i in (2, 1, 3):
         push(TB.at[0], TB.at[i], tb_s.at[i], tb_r.at[i], bdev[i])
     for i in range(1, 4):
         got(TB.at[i], tb_r.at[i])
     top, total = combine([TB[i, 0:1, :] for i in range(4)], [TB[i, 1:2, :] for i in range(4)])
-    lse = to_col(top + jnp.log(total), rows_g)
-    LS[q, 0:1, :] = to_row(lse, 256)
-    for d in (1, 2, 3):
+    lse_row = top + jnp.log(total)
+    LS[q, 0:1, :] = lse_row
+    for d in (2, 1, 3):
         push(LS.at[q], LS.at[q], ls_s.at[d - 1], ls_r.at[d - 1], zdev[d])
-    shift = score - lse
+    shift = score - to_col(lse_row, rows_g)
     outs = []
     for p in range(2 * n_pieces):
         CN[:, cols_of(p)] = (S[3 * rows_g:4 * rows_g, cols_of(p)] + CN[:, cols_of(p)] + shift) * inverse

time: 92.7 us -> 92.6 us (level)
  no operation moved by 1% of the time
where the time goes in v6:
time: 92.6 us; the launch traced here: 92.5 us
  Pallas kernels  88.5 us (96%)
  local copies, waits for them, and re-layouts  3.29 us (4%)
    pallas_call x1, Pallas kernels, call(): pl.pallas_call(kernel, out_shape=(jax.ShapeDtypeStruct((rows_g, voc), F32...  88.5 us
    unnamed x4, local copies, waits for them, and re-layouts  3.29 us

profile of v6, /device:TPU:0, one launch (start us, length us, event | category | flops | bytes accessed | tf_op | source)
XLA Modules:
  0.0 92.5 jit_solution(11537298908477026374)
XLA Ops:
  0.6 88.5 %shard_map.95 = (f32[192,2048]{1,0:T(8,128)}, f32[288]{0:T(512)}) custom-call(bf16[9,16384]{1,0:T(8,128)(2,1)} %hidden.1, bf16[2048,4096]{1,0:T(8,128)(2,1)} %head.1, f32[1,2048]{1,0:T(1,128)} %bitcast.3, s32[4]{0:T(128)} %live_in.1, s32[768]{0:T(1024)} %order_in.1, f32[288]{0:T(512)} %blp_in.1, s32[288]{0:T(512)} %tlen_in.1, s32[16,192]{1,0:T(8,128)} %bitcast.2), custom_call_target="tpu_custom_call" | custom-call | tf_op jit(solution)/shard_map/pallas_call | solution.py:459
  89.2 0.0 copy-start
  89.2 2.7 %copy.12 = f32[192,2048]{1,0:T(8,128)} copy(f32[192,2048]{1,0:T(8,128)} %get-tuple-element.4) | data formatting | bytes 3145728
  91.9 0.0 copy-done
  91.9 0.6 copy.13
Async XLA Ops:
  89.2 2.7 %copy-start = (f32[288]{0:T(512)S(1)}, f32[288]{0:T(512)}, u32[]{:S(2)}) copy-start(f32[288]{0:T(512)} %get-tuple-element.5) | copy-start | bytes 3460
